TPU v7x, 256 devices: a whole 4x4x8 slice. The times are simulated.
256 devices in a mesh: lon: 32 (over y_lo, z, core), lev: 8 (over x, y_hi).
Axes of the slice: x: 4, y: 4 (y_hi: 2, y_lo: 2; y = y_hi * 2 + y_lo), z: 8, core: 2. Of those that a mesh axis runs over, the one named last changes fastest.
Arguments:
- query_level: bfloat16 [8, 32, 128, 1024], P('lev', None, 'lon'), may hold values from -45 to 45
- key_level: bfloat16 [8, 32, 128, 1024], P('lev', None, 'lon'), may hold values from -15 to 15
- value_level: bfloat16 [8, 32, 128, 1024], P('lev', None, 'lon'), may hold values from -6 to 6
- block_lists: int32 [32, 4, 15], P('lon'), may hold values from 0 to 23, as said below
- query_column: bfloat16 [8, 32, 128, 1024], P(None, 'lev', 'lon'), may hold values from -45 to 45
- key_column: bfloat16 [8, 32, 128, 1024], P(None, 'lev', 'lon'), may hold values from -15 to 15
- grad_output: bfloat16 [8, 32, 128, 1024], P(None, 'lev', 'lon'), may hold values from -6 to 6
Outputs:
- grad_query_level: bfloat16 [8, 32, 128, 1024], P('lev', None, 'lon')
- grad_key_level: bfloat16 [8, 32, 128, 1024], P('lev', None, 'lon')
- grad_value_level: bfloat16 [8, 32, 128, 1024], P('lev', None, 'lon')
- grad_query_column: bfloat16 [8, 32, 128, 1024], P(None, 'lev', 'lon')
- grad_key_column: bfloat16 [8, 32, 128, 1024], P(None, 'lev', 'lon')
Inputs may be any that keep to these rules, and one draw needn't show every extreme that they name: `block_lists`: the entries of one row are distinct key blocks of the tile's extended region, and every row lists the two key blocks that lie under its own query block.
All inputs are finite; a program needn't handle non-finite values.
Results may differ from a plain program's by a relative error of at most 0.0072.
Values may be sent and summed in bfloat16 or wider, within the bound.
No kernel may reach another device: no remote copies, remote signals or barrier semaphores. Data moves between devices by JAX's collectives and lax.ppermute only.
A program may use at most 64 MiB of HBM per device.

v0:
```python
import math

import jax
import jax.numpy as jnp
from jax import lax
from jax.sharding import PartitionSpec as P

HEADS = 16
HALO = 4


NEGATIVE = -1e30
heads_per_group = 4


def padded(array, sides, width):
    for axis, dim in sides:
        size, length = (lax.axis_size(axis), array.shape[dim])
        up = [(i, (i + 1) % size) for i in range(size)]
        down = [(j, i) for i, j in up]
        last = lax.slice_in_dim(array, length - width, length, axis=dim)
        first = lax.slice_in_dim(array, 0, width, axis=dim)
        before = lax.ppermute(last, axis, up)
        after = lax.ppermute(first, axis, down)
        array = jnp.concatenate([before, array, after], axis=dim)
    return array


def from_behind(block, axis, distance):
    devices = range(lax.axis_size(axis))
    route = [((i - distance) % len(devices), i) for i in devices]
    return lax.ppermute(block, axis, route)


def token_mask(list_rows, lat_rows, lon_dev, extent):
    key_blocks = lat_rows // 8 * (extent // 2)
    block_ids = jnp.arange(key_blocks, dtype=jnp.int32)
    listed = jnp.any(list_rows[:, :, None] == block_ids[None, None, :], axis=1)
    listed = listed.reshape(lat_rows // 8, lon_dev // 4, lat_rows // 8, extent // 2)
    spread = jnp.broadcast_to(
        listed[:, None, :, None, :, None, :, None],
        (lat_rows // 8, 8, lon_dev // 4, 4, lat_rows // 8, 8, extent // 2, 2),
    )
    return spread.reshape(lat_rows * lon_dev, lat_rows * extent)


def masked_softmax(scores, allowed):
    scores = jnp.where(allowed, scores, NEGATIVE)
    row_max = jnp.max(scores, axis=-1, keepdims=True)
    raised = jnp.exp(scores - row_max)
    return raised / jnp.sum(raised, axis=-1, keepdims=True)


def plain_softmax(scores):
    row_max = jnp.max(scores, axis=-1, keepdims=True)
    raised = jnp.exp(scores - row_max)
    return raised / jnp.sum(raised, axis=-1, keepdims=True)


def on_device(
    query_level, key_level, value_level, block_lists, query_column, key_column, grad_output
):
    levels_dev, lat_rows, lon_dev, model_width = query_level.shape
    extent = lon_dev + 2 * HALO
    head_dim = model_width // HEADS
    scaling = 1.0 / math.sqrt(head_dim)
    head_group = min(heads_per_group, HEADS)
    group_count = HEADS // head_group
    group_width = head_group * head_dim
    query_count = lat_rows * lon_dev
    rim_count = lat_rows * HALO
    grid_mask = token_mask(block_lists[0], lat_rows, lon_dev, extent).reshape(
        query_count, lat_rows, extent
    )
    allowed = jnp.concatenate(
        [
            grid_mask[:, :, :HALO].reshape(query_count, rim_count),
            grid_mask[:, :, HALO : HALO + lon_dev].reshape(query_count, query_count),
            grid_mask[:, :, HALO + lon_dev :].reshape(query_count, rim_count),
        ],
        axis=1,
    )
    stacked = jnp.stack([key_level, value_level])
    extended = padded(stacked, (("lon", 3),), HALO)

    def flatten_pair(part):
        return part.reshape(2, levels_dev, -1, model_width)

    left_pair = flatten_pair(extended[:, :, :, :HALO])
    right_pair = flatten_pair(extended[:, :, :, HALO + lon_dev :])
    own_pair = flatten_pair(stacked)
    ordered = jnp.concatenate([left_pair, own_pair, right_pair], axis=2)
    keys_all = ordered[0]
    values_all = ordered[1]
    queries = query_level.reshape(levels_dev, query_count, model_width)

    def group_cut(array, group):
        piece = array[..., group * group_width : (group + 1) * group_width]
        return piece.reshape(piece.shape[:-1] + (head_group, head_dim))

    def scores_of(group):
        query_part = group_cut(queries, group)
        pieces = (group_cut(keys_all, group),)
        products = [
            jnp.einsum("lqhd,lkhd->lhqk", query_part, piece, preferred_element_type=jnp.float32)
            for piece in pieces
        ]
        return products[0] * scaling

    attended_parts = []
    for group in range(group_count):
        attn_probs = masked_softmax(scores_of(group), allowed)
        attend_value_part = group_cut(values_all, group)
        mixed = jnp.einsum(
            "lhqk,lkhd->lqhd",
            attn_probs.astype(jnp.bfloat16),
            attend_value_part,
            preferred_element_type=jnp.float32,
        )
        attended_parts.append(
            mixed.astype(jnp.bfloat16).reshape(levels_dev, query_count, group_width)
        )
    attended = jnp.concatenate(attended_parts, axis=-1).reshape(
        levels_dev, lat_rows, lon_dev, model_width
    )
    columns = lax.all_to_all(attended, "lev", split_axis=1, concat_axis=0, tiled=True)
    column_levels = columns.shape[0]
    lat_col = columns.shape[1]

    def column_heads(array):
        return array.reshape(column_levels, lat_col * lon_dev, HEADS, head_dim)

    col_query = column_heads(query_column)
    col_key = column_heads(key_column)
    col_grad = column_heads(grad_output)
    col_att = column_heads(columns)
    col_probs = plain_softmax(
        jnp.einsum("lthd,mthd->thlm", col_query, col_key, preferred_element_type=jnp.float32)
        * scaling
    )
    d_col_probs = jnp.einsum(
        "lthd,mthd->thlm", col_grad, col_att, preferred_element_type=jnp.float32
    )
    d_col_scores = col_probs * (
        d_col_probs - jnp.sum(col_probs * d_col_probs, axis=-1, keepdims=True)
    )
    col_scores_b = d_col_scores.astype(jnp.bfloat16)
    grad_query_column = (
        (
            jnp.einsum("thlm,mthd->lthd", col_scores_b, col_key, preferred_element_type=jnp.float32)
            * scaling
        )
        .astype(jnp.bfloat16)
        .reshape(query_column.shape)
    )
    grad_key_column = (
        (
            jnp.einsum(
                "thlm,lthd->mthd", col_scores_b, col_query, preferred_element_type=jnp.float32
            )
            * scaling
        )
        .astype(jnp.bfloat16)
        .reshape(key_column.shape)
    )
    grad_col = (
        jnp.einsum(
            "thlm,lthd->mthd",
            col_probs.astype(jnp.bfloat16),
            col_grad,
            preferred_element_type=jnp.float32,
        )
        .astype(jnp.bfloat16)
        .reshape(columns.shape)
    )
    grad_attended = lax.all_to_all(grad_col, "lev", split_axis=0, concat_axis=1, tiled=True)
    grad_flat = grad_attended.reshape(levels_dev, query_count, model_width)
    query_grads = []
    key_grads = []
    value_grads = []
    for group in range(group_count):
        attn_probs = masked_softmax(scores_of(group), allowed)
        probs_b = attn_probs.astype(jnp.bfloat16)
        query_part = group_cut(queries, group)
        key_part = group_cut(keys_all, group)
        value_part = group_cut(values_all, group)
        grad_part = group_cut(grad_flat, group)
        d_probs = jnp.einsum(
            "lqhd,lkhd->lhqk", grad_part, value_part, preferred_element_type=jnp.float32
        )
        d_scores = attn_probs * (d_probs - jnp.sum(attn_probs * d_probs, axis=-1, keepdims=True))
        scores_b = d_scores.astype(jnp.bfloat16)
        grad_query = (
            jnp.einsum("lhqk,lkhd->lqhd", scores_b, key_part, preferred_element_type=jnp.float32)
            * scaling
        )
        key_terms = (
            jnp.einsum("lhqk,lqhd->lkhd", scores_b, query_part, preferred_element_type=jnp.float32)
            * scaling
        )
        value_terms = jnp.einsum(
            "lhqk,lqhd->lkhd", probs_b, grad_part, preferred_element_type=jnp.float32
        )
        query_grads.append(
            grad_query.astype(jnp.bfloat16).reshape(levels_dev, query_count, group_width)
        )
        key_grads.append(key_terms.reshape(levels_dev, -1, group_width))
        value_grads.append(value_terms.reshape(levels_dev, -1, group_width))
    grad_query_level = jnp.concatenate(query_grads, axis=-1).reshape(
        levels_dev, lat_rows, lon_dev, model_width
    )
    grad_terms = jnp.stack(
        [jnp.concatenate(key_grads, axis=-1), jnp.concatenate(value_grads, axis=-1)]
    )
    interior = grad_terms[:, :, rim_count : rim_count + query_count].reshape(
        2, levels_dev, lat_rows, lon_dev, model_width
    )
    left_rim = (
        grad_terms[:, :, :rim_count]
        .reshape(2, levels_dev, lat_rows, HALO, model_width)
        .astype(jnp.bfloat16)
    )
    right_rim = (
        grad_terms[:, :, rim_count + query_count :]
        .reshape(2, levels_dev, lat_rows, HALO, model_width)
        .astype(jnp.bfloat16)
    )
    from_right = from_behind(left_rim, "lon", -1)
    from_left = from_behind(right_rim, "lon", 1)
    summed = interior.at[:, :, :, :HALO].add(from_left.astype(jnp.float32))
    summed = summed.at[:, :, :, lon_dev - HALO :].add(from_right.astype(jnp.float32))
    summed = summed.astype(jnp.bfloat16)
    return (grad_query_level, summed[0], summed[1], grad_query_column, grad_key_column)


def solution(mesh):
    placed = (
        P("lev", None, "lon", None),
        P("lev", None, "lon", None),
        P("lev", None, "lon", None),
        P("lon", None, None),
        P(None, "lev", "lon", None),
        P(None, "lev", "lon", None),
        P(None, "lev", "lon", None),
    )
    return jax.shard_map(
        on_device,
        mesh=mesh,
        in_specs=placed,
        out_specs=(
            P("lev", None, "lon", None),
            P("lev", None, "lon", None),
            P("lev", None, "lon", None),
            P(None, "lev", "lon", None),
            P(None, "lev", "lon", None),
        ),
        check_vma=False,
    )
```

profile of v0, /device:TPU:2, one launch (start us, length us, event | category | flops | bytes accessed | tf_op | source)
XLA Modules:
  0.0 93.6 jit_solution(13050121807752547266)
XLA Ops:
  0.7 1.5 %pad_maximum_fusion.2 = bf16[2,1,32,4,1024]{4,3,2,1,0:T(4,128)(2,1)S(1)} fusion(bf16[1,1,32,4,1024]{4,3,2,1,0:T(4,128)(2,1)} %bitcast.281, bf16[1,1,32,4,1024]{4,3,2,1,0:T(4,128)(2,1)} %bitcast.280), kind=kLoop, calls=%fused_computation.82 | loop fusion | flops 262144 | bytes 1048576 | tf_op jit(solution)/shard_map/stack | solution.py:83
  2.2 6.4 %collective-permute-start.1 = (bf16[2,1,32,4,1024]{4,3,2,1,0:T(4,128)(2,1)S(1)}, bf16[2,1,32,4,1024]{4,3,2,1,0:T(4,128)(2,1)}, u32[]{:S(2)}, u32[]{:S(2)}) collective-permute-start(bf16[2,1,32,4,1024]{4,3,2,1,0:T(4,128)(2,1)S(1)} %pad_maximum_fusion.2), channel_id=1, source_target_pairs={{8,0},{16,8},{24,16},{32,24},{40,32},{48,40},{56,48},{64,56},{72,6... | collective-permute-start | bytes 1572872 | tf_op jit(solution)/shard_map/ppermute | solution.py:24
  8.6 1.3 %reshape.564 = bf16[8,16,16,64]{3,2,1,0:T(8,128)(2,1)S(1)} reshape(bf16[8,4,4,1024]{3,2,1,0:T(4,128)(2,1)} %param.19) | data formatting | bytes 524288 | tf_op jit(solution)/shard_map/reshape | solution.py:131
  9.9 0.4 reshape.565
  10.3 0.4 reshape.566
  10.7 1.1 %fusion.91 = (f32[16,16,8]{2,1,0:T(8,128)S(1)}, f32[16,16,8,8]{2,3,1,0:T(8,128)S(1)}) fusion(bf16[8,16,16,64]{3,2,1,0:T(8,128)(2,1)S(1)} %reshape.565, bf16[8,16,16,64]{3,2,1,0:T(8,128)(2,1)S(1)} %reshape.564), kind=kOutput, calls=%fused_computation.135 | convolution fusion | flops 2146311 | bytes 598016 | tf_op jit(solution)/shard_map/sub | solution.py:56
  11.9 0.5 fusion.28
  12.4 0.4 copy-done.10
  12.9 1.0 %reshape.595 = bf16[8,4,4,1024]{3,2,1,0:T(4,128)(2,1)} reshape(bf16[8,16,16,64]{3,2,1,0:T(8,128)(2,1)S(1)} %copy.340) | data formatting | bytes 524288 | tf_op jit(solution)/shard_map/reshape | solution.py:174
  13.9 7.2 %all-to-all-start = ((bf16[8,4,4,1024]{3,2,1,0:T(4,128)(2,1)}), bf16[8,4,4,1024]{3,2,1,0:T(4,128)(2,1)S(1)}, u32[]{:S(2)}, u32[]{:S(2)}) async-start(bf16[8,4,4,1024]{3,2,1,0:T(4,128)(2,1)} %reshape.595), calls=%async_computation | async-start | bytes 524288 | tf_op jit(solution)/shard_map/all_to_all | solution.py:176
  21.5 0.5 broadcast_in_dim.27
  22.0 0.9 reshape_reshape.3
  24.1 0.7 copy.347
  25.1 2.7 %all-to-all-done = bf16[8,4,4,1024]{3,2,1,0:T(4,128)(2,1)S(1)} async-done(((bf16[8,4,4,1024]{3,2,1,0:T(4,128)(2,1)}), bf16[8,4,4,1024]{3,2,1,0:T(4,128)(2,1)S(1)}, u32[]{:S(2)}, u32[]{:S(2)}) %all-to-all-start) | async-done | bytes 262176 | tf_op jit(solution)/shard_map/all_to_all | solution.py:176
  28.0 0.7 copy.273
  28.7 0.7 copy.279
  29.4 0.7 copy.285
  30.2 1.2 %reshape.556 = bf16[2,1,128,1024]{3,2,0,1:T(8,128)(2,1)S(1)} reshape(bf16[2,1,32,4,1024]{4,3,2,1,0:T(4,128)(2,1)} %collective-permute-done) | data formatting | bytes 1048576 | tf_op jit(solution)/shard_map/reshape | solution.py:87
  31.6 1.2 %reshape.557 = bf16[2,1,128,1024]{3,2,0,1:T(8,128)(2,1)S(1)} reshape(bf16[2,1,32,4,1024]{4,3,2,1,0:T(4,128)(2,1)} %collective-permute-done.1) | data formatting | bytes 1048576 | tf_op jit(solution)/shard_map/reshape | solution.py:87
  33.4 0.9 fusion.86
  34.4 0.5 fusion.99
  34.8 1.2 %fusion.37 = bf16[1,128,4,64]{1,3,2,0:T(8,128)(2,1)} fusion(bf16[384,4,64]{0,2,1:T(8,128)(2,1)S(1)} %bitcast.324, f32[4,128]{1,0:T(4,128)S(1)} %get-tuple-element.104, bf16[384,4,64]{0,2,1:T(8,128)(2,1)S(1)} %bitcast.295, bf16[128,4,64]{0,2,1:T(8,128)(2,1)S(1)} %bitcast.315, pred[128,384]{0,1:T(8,128)(4,1)S(1)} %pad_add_fusion), kind=kOutput, calls=%fused_computation.64 | convolution fusion | flops 51348352 | bytes 575488 | tf_op jit(solution)/shard_map/lhqk,lkhd->lqhd/dot_general | solution.py:114
  36.1 1.4 %fusion.60 = f32[4,64,384]{2,1,0:T(8,128)} fusion(bf16[128,4,64]{0,2,1:T(8,128)(2,1)S(1)} %bitcast.332, f32[4,128]{1,0:T(4,128)S(1)} %get-tuple-element.104, bf16[384,4,64]{0,2,1:T(8,128)(2,1)S(1)} %bitcast.296, bf16[128,4,64]{0,2,1:T(8,128)(2,1)S(1)} %bitcast.316, pred[128,384]{0,1:T(8,128)(4,1)S(1)} %pad_add_fusion), kind=kOutput, calls=%fused_computation.110 | convolution fusion | flops 51315584 | bytes 772096 | tf_op jit(solution)/shard_map/lhqk,lqhd->lkhd/dot_general | solution.py:201
  37.5 1.2 %multiply_reduce_fusion.4 = (f32[4,128]{1,0:T(4,128)S(1)}, f32[4,128,384]{1,2,0:T(8,128)S(1)}) fusion(f32[4,128,384]{1,2,0:T(8,128)S(1)} %get-tuple-element.105, f32[4,128]{1,0:T(4,128)S(1)} %get-tuple-element.104, bf16[128,4,64]{0,2,1:T(8,128)(2,1)} %bitcast.333, bf16[384,4,64]{0,2,1:T(8,128)(2,1)S(1)} %bitcast.325), kind=kOutput, calls=%fused_computation.81 | convolution fusion | flops 25755136 | bytes 1839104 | tf_op jit(solution)/shard_map/lqhd,lkhd->lhqk/dot_general | solution.py:188
  38.8 0.7 copy-done.32
  39.8 0.5 fusion.98
  40.3 1.2 %fusion.38 = bf16[1,128,4,64]{1,3,2,0:T(8,128)(2,1)} fusion(bf16[384,4,64]{0,2,1:T(8,128)(2,1)S(1)} %bitcast.322, f32[4,128]{1,0:T(4,128)S(1)} %get-tuple-element.100, bf16[384,4,64]{0,2,1:T(8,128)(2,1)S(1)} %bitcast.291, bf16[128,4,64]{0,2,1:T(8,128)(2,1)S(1)} %bitcast.311, pred[128,384]{0,1:T(8,128)(4,1)S(1)} %copy-done.46), kind=kOutput, calls=%fused_computation.65 | convolution fusion | flops 51348352 | bytes 575488 | tf_op jit(solution)/shard_map/lhqk,lkhd->lqhd/dot_general | solution.py:114
  41.5 1.4 %fusion.57 = f32[4,64,384]{2,1,0:T(8,128)} fusion(bf16[128,4,64]{0,2,1:T(8,128)(2,1)S(1)} %bitcast.330, f32[4,128]{1,0:T(4,128)S(1)} %get-tuple-element.100, bf16[384,4,64]{0,2,1:T(8,128)(2,1)S(1)} %bitcast.292, bf16[128,4,64]{0,2,1:T(8,128)(2,1)S(1)} %bitcast.312, pred[128,384]{0,1:T(8,128)(4,1)S(1)} %copy-done.46), kind=kOutput, calls=%fused_computation.107 | convolution fusion | flops 51315584 | bytes 772096 | tf_op jit(solution)/shard_map/lhqk,lqhd->lkhd/dot_general | solution.py:201
  43.4 0.7 copy-done
  44.4 1.3 %fusion.97 = (f32[4,128]{1,0:T(4,128)S(1)}, f32[4,128,384]{1,2,0:T(8,128)S(1)}) fusion(bf16[384,4,64]{0,2,1:T(8,128)(2,1)S(1)} %bitcast.286, bf16[128,4,64]{0,2,1:T(8,128)(2,1)S(1)} %bitcast.306, pred[128,384]{0,1:T(8,128)(4,1)} %copy-done.45), kind=kOutput, calls=%fused_computation.137 | convolution fusion | flops 25952640 | bytes 1099776 | tf_op jit(solution)/shard_map/sub | solution.py:50
  45.7 2.1 %fusion.39 = bf16[1,128,4,64]{1,3,2,0:T(8,128)(2,1)} fusion(bf16[384,4,64]{0,2,1:T(8,128)(2,1)S(1)} %bitcast.320, f32[4,128]{1,0:T(4,128)S(1)} %get-tuple-element.96, bf16[384,4,64]{0,2,1:T(8,128)(2,1)S(1)} %bitcast.287, bf16[128,4,64]{0,2,1:T(8,128)(2,1)S(1)} %bitcast.307, pred[128,384]{0,1:T(8,128)(4,1)} %copy-done.45), kind=kOutput, calls=%fused_computation.66 | convolution fusion | flops 51348352 | bytes 575488 | tf_op jit(solution)/shard_map/lhqk,lkhd->lqhd/dot_general | solution.py:114
  47.8 2.2 %fusion.54 = f32[4,64,384]{2,1,0:T(8,128)} fusion(bf16[128,4,64]{0,2,1:T(8,128)(2,1)S(1)} %bitcast.328, f32[4,128]{1,0:T(4,128)S(1)} %get-tuple-element.96, bf16[384,4,64]{0,2,1:T(8,128)(2,1)S(1)} %bitcast.288, bf16[128,4,64]{0,2,1:T(8,128)(2,1)S(1)} %bitcast.308, pred[128,384]{0,1:T(8,128)(4,1)} %copy-done.45), kind=kOutput, calls=%fused_computation.104 | convolution fusion | flops 51315584 | bytes 772096 | tf_op jit(solution)/shard_map/lhqk,lqhd->lkhd/dot_general | solution.py:201
  50.4 0.8 copy-done.2
  51.5 0.5 fusion.96
  52.1 1.2 %fusion.40 = bf16[1,128,4,64]{1,3,2,0:T(8,128)(2,1)} fusion(bf16[384,4,64]{0,2,1:T(8,128)(2,1)S(1)} %bitcast.318, f32[4,128]{1,0:T(4,128)S(1)} %get-tuple-element.92, bf16[384,4,64]{0,2,1:T(8,128)(2,1)S(1)} %bitcast.283, bf16[128,4,64]{0,2,1:T(8,128)(2,1)S(1)} %bitcast.303, pred[128,384]{0,1:T(8,128)(4,1)S(1)} %copy-done.47), kind=kOutput, calls=%fused_computation.67 | convolution fusion | flops 51348352 | bytes 575488 | tf_op jit(solution)/shard_map/lhqk,lkhd->lqhd/dot_general | solution.py:114
  53.4 1.4 %fusion.51 = f32[4,64,384]{2,1,0:T(8,128)} fusion(bf16[128,4,64]{0,2,1:T(8,128)(2,1)S(1)} %bitcast.326, f32[4,128]{1,0:T(4,128)S(1)} %get-tuple-element.92, bf16[384,4,64]{0,2,1:T(8,128)(2,1)S(1)} %bitcast.284, bf16[128,4,64]{0,2,1:T(8,128)(2,1)S(1)} %bitcast.304, pred[128,384]{0,1:T(8,128)(4,1)S(1)} %copy-done.47), kind=kOutput, calls=%fused_computation.101 | convolution fusion | flops 51315584 | bytes 772096 | tf_op jit(solution)/shard_map/lhqk,lqhd->lkhd/dot_general | solution.py:201
  54.8 0.3 multiply_reduce_fusion.1
  55.7 0.8 copy-done.22
  57.1 0.5 fusion.5
  57.6 0.4 copy-done.19
  58.0 0.9 fusion.36
  58.9 0.8 fusion.35
  59.7 0.8 fusion.34
  61.8 0.8 maximum_bitcast_fusion.2
  62.6 5.7 %all-to-all-start.1 = ((bf16[1,32,4,1024]{3,2,0,1:T(4,128)(2,1)}), bf16[1,32,4,1024]{3,2,0,1:T(4,128)(2,1)}, u32[]{:S(2)}, u32[]{:S(2)}) async-start(bf16[1,32,4,1024]{3,2,0,1:T(4,128)(2,1)} %maximum_bitcast_fusion.2), calls=%async_computation.1 | async-start | bytes 524288 | tf_op jit(solution)/shard_map/all_to_all | solution.py:126
  68.3 1.4 %copy.298 = f32[2,1,128,1024]{3,2,0,1:T(8,128)} copy(f32[2,1,128,1024]{2,3,1,0:T(8,128)S(1)} %fusion.41) | data formatting | bytes 2097152 | tf_op jit(solution)/shard_map/slice | solution.py:215
  69.7 1.5 %reshape.591 = f32[2,1,32,4,1024]{4,3,2,1,0:T(4,128)S(1)} reshape(f32[2,1,128,1024]{3,2,0,1:T(8,128)} %copy.298) | data formatting | bytes 2097152 | tf_op jit(solution)/shard_map/reshape | solution.py:215
  71.2 1.0 %fusion.85 = (bf16[2,1,128,1024]{2,3,1,0:T(8,128)(2,1)}, bf16[2,1,128,1024]{2,3,1,0:T(8,128)(2,1)S(1)}) fusion(bf16[2,1,384,1024]{2,3,1,0:T(8,128)(2,1)S(1)} %fusion.5), kind=kLoop, calls=%fused_computation.129 | loop fusion | bytes 2097152 | tf_op jit(solution)/shard_map/slice | solution.py:224
  72.2 1.2 %copy.299 = bf16[2,1,128,1024]{3,2,0,1:T(8,128)(2,1)S(1)} copy(bf16[2,1,128,1024]{2,3,1,0:T(8,128)(2,1)} %get-tuple-element.65) | data formatting | bytes 1048576 | tf_op jit(solution)/shard_map/slice | solution.py:224
  73.5 1.0 %convert_element_type.190 = bf16[2,1,32,4,1024]{4,3,2,1,0:T(4,128)(2,1)} reshape(bf16[2,1,128,1024]{3,2,0,1:T(8,128)(2,1)S(1)} %copy.299) | data formatting | bytes 1048576 | tf_op jit(solution)/shard_map/convert_element_type | solution.py:226
  74.7 1.0 %convert_element_type.192 = bf16[2,1,32,4,1024]{4,3,2,1,0:T(4,128)(2,1)} reshape(bf16[2,1,128,1024]{3,2,0,1:T(8,128)(2,1)S(1)} %copy.300) | data formatting | bytes 1048576 | tf_op jit(solution)/shard_map/convert_element_type | solution.py:221
  75.7 3.9 %collective-permute-start.3 = (bf16[2,1,32,4,1024]{4,3,2,1,0:T(4,128)(2,1)}, bf16[2,1,32,4,1024]{4,3,2,1,0:T(4,128)(2,1)}, u32[]{:S(2)}, u32[]{:S(2)}) collective-permute-start(bf16[2,1,32,4,1024]{4,3,2,1,0:T(4,128)(2,1)} %convert_element_type.192), channel_id=1, source_target_pairs={{8,0},{16,8},{24,16},{32,24},{40,32},{48,40},{56,48},{64,56},{72,6... | collective-permute-start | bytes 1572872 | tf_op jit(solution)/shard_map/ppermute | solution.py:32
  79.9 1.1 %copy.277 = bf16[1,128,4,64]{3,2,1,0:T(4,128)(2,1)S(1)} copy(bf16[1,128,4,64]{1,3,2,0:T(8,128)(2,1)} %fusion.35) | data formatting | bytes 131072 | tf_op jit(solution)/shard_map/convert_element_type | solution.py:205
  81.1 1.0 %copy.283 = bf16[1,128,4,64]{3,2,1,0:T(4,128)(2,1)S(1)} copy(bf16[1,128,4,64]{1,3,2,0:T(8,128)(2,1)} %fusion.34) | data formatting | bytes 131072 | tf_op jit(solution)/shard_map/convert_element_type | solution.py:205
  82.8 0.8 pad_maximum_fusion.3
  83.6 1.3 %reshape.592 = bf16[8,16,16,64]{3,2,1,0:T(8,128)(2,1)S(1)} reshape(bf16[1,32,4,1024]{3,2,0,1:T(4,128)(2,1)} %all-to-all-done.1) | data formatting | bytes 524288 | tf_op jit(solution)/shard_map/reshape | solution.py:131
  85.0 1.9 %multiply_reduce_fusion = (f32[16,16,8]{2,1,0:T(8,128)S(1)}, f32[16,16,8,8]{2,3,1,0:T(8,128)S(1)}) fusion(f32[16,16,8,8]{2,3,1,0:T(8,128)S(1)} %copy-done.11, f32[16,16,8]{2,1,0:T(8,128)} %copy-done.35, bf16[8,16,16,64]{3,2,1,0:T(8,128)(2,1)S(1)} %copy-done.21, bf16[8,16,16,64]{3,2,1,0:T(8,128)(2,1)S(1)} %reshape.592), kind=kOutput, calls=%fused_computation.70 | convolution fusion | flops 2144256 | bytes 671744 | tf_op jit(solution)/shard_map/lthd,mthd->thlm/dot_general | solution.py:141
  87.2 0.7 copy-done.7
  87.9 0.5 fusion.26
  88.5 1.0 %reshape.597 = bf16[8,4,4,1024]{3,2,1,0:T(4,128)(2,1)} reshape(bf16[8,16,16,64]{3,2,1,0:T(8,128)(2,1)S(1)} %copy.342) | data formatting | bytes 524288
  89.4 0.5 fusion.27
  90.1 1.0 %reshape.596 = bf16[8,4,4,1024]{3,2,1,0:T(4,128)(2,1)} reshape(bf16[8,16,16,64]{3,2,1,0:T(8,128)(2,1)S(1)} %copy.341) | data formatting | bytes 524288
  91.1 1.6 %add_convert_fusion = bf16[2,1,32,4,1024]{4,3,2,1,0:T(4,128)(2,1)S(1)} fusion(bf16[2,1,32,4,1024]{4,3,2,1,0:T(4,128)(2,1)} %collective-permute-done.3, f32[2,1,32,4,1024]{4,3,2,1,0:T(4,128)S(1)} %reshape.591, bf16[2,1,32,4,1024]{4,3,2,1,0:T(4,128)(2,1)} %collective-permute-done.2), kind=kLoop, calls=%fused_computation.71 | loop fusion | flops 1310720 | bytes 2621440 | tf_op jit(solution)/shard_map/convert_element_type | solution.py:232
  92.7 1.0 %slice_bitcast_fusion.2 = (bf16[1,32,4,1024]{3,2,1,0:T(4,128)(2,1)}, bf16[1,32,4,1024]{3,2,1,0:T(4,128)(2,1)}) fusion(bf16[2,1,32,4,1024]{4,3,2,1,0:T(4,128)(2,1)S(1)} %add_convert_fusion), kind=kLoop, calls=%fused_computation.96 | loop fusion | bytes 1048576 | tf_op jit(solution)/shard_map/squeeze | solution.py:233
  (156 shorter events, 9.2 us)
Async XLA Ops:
  0.6 9.3 %copy-start.26 = (bf16[8,4,4,1024]{3,2,1,0:T(4,128)(2,1)S(1)}, bf16[8,4,4,1024]{3,2,1,0:T(4,128)(2,1)}, u32[]{:S(2)}) copy-start(bf16[8,4,4,1024]{3,2,1,0:T(4,128)(2,1)} %param.20) | copy-start | bytes 786436
  0.6 9.7 %copy-start.27 = (bf16[8,4,4,1024]{3,2,1,0:T(4,128)(2,1)S(1)}, bf16[8,4,4,1024]{3,2,1,0:T(4,128)(2,1)}, u32[]{:S(2)}) copy-start(bf16[8,4,4,1024]{3,2,1,0:T(4,128)(2,1)} %param.21) | copy-start | bytes 786436
  2.1 28.0 %collective-permute-start = (bf16[2,1,32,4,1024]{4,3,2,1,0:T(4,128)(2,1)S(1)}, bf16[2,1,32,4,1024]{4,3,2,1,0:T(4,128)(2,1)}, u32[]{:S(2)}, u32[]{:S(2)}) collective-permute-start(bf16[2,1,32,4,1024]{4,3,2,1,0:T(4,128)(2,1)S(1)} %pad_maximum_fusion.2), channel_id=1, source_target_pairs={{0,8},{8,16},{16,24},{24,32},{32,40},{40,48},{48,56},{56,64},{64,7... | collective-permute-start | bytes 1572872 | tf_op jit(solution)/shard_map/ppermute | solution.py:23
  2.2 29.4 %collective-permute-start.1 = (bf16[2,1,32,4,1024]{4,3,2,1,0:T(4,128)(2,1)S(1)}, bf16[2,1,32,4,1024]{4,3,2,1,0:T(4,128)(2,1)}, u32[]{:S(2)}, u32[]{:S(2)}) collective-permute-start(bf16[2,1,32,4,1024]{4,3,2,1,0:T(4,128)(2,1)S(1)} %pad_maximum_fusion.2), channel_id=1, source_target_pairs={{8,0},{16,8},{24,16},{32,24},{40,32},{48,40},{56,48},{64,56},{72,6... | collective-permute-start | bytes 1572872 | tf_op jit(solution)/shard_map/ppermute | solution.py:24
  9.9 1.9 %copy-start.6 = (bf16[8,16,16,64]{3,2,1,0:T(8,128)(2,1)}, bf16[8,16,16,64]{3,2,1,0:T(8,128)(2,1)S(1)}, u32[]{:S(2)}) copy-start(bf16[8,16,16,64]{3,2,1,0:T(8,128)(2,1)S(1)} %reshape.564) | copy-start | bytes 786436
  10.3 1.5 %copy-start.4 = (bf16[8,16,16,64]{3,2,1,0:T(8,128)(2,1)}, bf16[8,16,16,64]{3,2,1,0:T(8,128)(2,1)S(1)}, u32[]{:S(2)}) copy-start(bf16[8,16,16,64]{3,2,1,0:T(8,128)(2,1)S(1)} %reshape.565) | copy-start | bytes 786436
  10.7 1.2 %copy-start.20 = (bf16[8,16,16,64]{3,2,1,0:T(8,128)(2,1)}, bf16[8,16,16,64]{3,2,1,0:T(8,128)(2,1)S(1)}, u32[]{:S(2)}) copy-start(bf16[8,16,16,64]{3,2,1,0:T(8,128)(2,1)S(1)} %reshape.566) | copy-start | bytes 786436
  11.8 1.0 %copy-start.10 = (f32[16,16,8,8]{2,3,1,0:T(8,128)}, f32[16,16,8,8]{2,3,1,0:T(8,128)S(1)}, u32[]{:S(2)}) copy-start(f32[16,16,8,8]{2,3,1,0:T(8,128)S(1)} %get-tuple-element.91) | copy-start | bytes 196612
  11.8 1.0 %copy-start.35 = (f32[16,16,8]{2,1,0:T(8,128)}, f32[16,16,8]{2,1,0:T(8,128)S(1)}, u32[]{:S(2)}) copy-start(f32[16,16,8]{2,1,0:T(8,128)S(1)} %get-tuple-element.90) | copy-start | bytes 24580
  12.8 8.2 %copy-start.48 = (s32[1,4,15]{2,1,0:T(4,128)S(1)}, s32[1,4,15]{2,1,0:T(4,128)}, u32[]{:S(2)}) copy-start(s32[1,4,15]{2,1,0:T(4,128)} %param.18) | copy-start | bytes 724
  12.9 10.0 %copy-start.29 = (bf16[1,32,4,1024]{3,2,1,0:T(4,128)(2,1)S(1)}, bf16[1,32,4,1024]{3,2,1,0:T(4,128)(2,1)}, u32[]{:S(2)}) copy-start(bf16[1,32,4,1024]{3,2,1,0:T(4,128)(2,1)} %param.15) | copy-start | bytes 786436
  13.9 13.8 %all-to-all-start = ((bf16[8,4,4,1024]{3,2,1,0:T(4,128)(2,1)}), bf16[8,4,4,1024]{3,2,1,0:T(4,128)(2,1)S(1)}, u32[]{:S(2)}, u32[]{:S(2)}) async-start(bf16[8,4,4,1024]{3,2,1,0:T(4,128)(2,1)} %reshape.595), calls=%async_computation | async-start | bytes 524288 | tf_op jit(solution)/shard_map/all_to_all | solution.py:176
  21.5 1.5 %copy-start.8 = (bf16[1,32,4,1024]{3,2,1,0:T(4,128)(2,1)S(1)}, bf16[1,32,4,1024]{3,2,1,0:T(4,128)(2,1)}, u32[]{:S(2)}) copy-start(bf16[1,32,4,1024]{3,2,1,0:T(4,128)(2,1)} %param.16) | copy-start | bytes 786436
  22.0 1.1 %copy-start.9 = (bf16[1,32,4,1024]{3,2,1,0:T(4,128)(2,1)S(1)}, bf16[1,32,4,1024]{3,2,1,0:T(4,128)(2,1)}, u32[]{:S(2)}) copy-start(bf16[1,32,4,1024]{3,2,1,0:T(4,128)(2,1)} %param.17) | copy-start | bytes 786436
  24.1 12.0 %copy-start.31 = (bf16[1,128,256]{1,2,0:T(8,128)(2,1)}, bf16[1,128,256]{1,2,0:T(8,128)(2,1)S(1)}, u32[]{:S(2)}) copy-start(bf16[1,128,256]{1,2,0:T(8,128)(2,1)S(1)} %copy.346) | copy-start | bytes 196612
  25.1 11.0 %copy-start.45 = (pred[128,384]{0,1:T(8,128)(4,1)}, pred[128,384]{0,1:T(8,128)(4,1)S(1)}, u32[]{:S(2)}) copy-start(pred[128,384]{0,1:T(8,128)(4,1)S(1)} %pad_add_fusion) | copy-start | bytes 147460
  28.0 8.1 %copy-start.44 = (bf16[1,128,256]{1,2,0:T(8,128)(2,1)}, bf16[1,128,256]{1,2,0:T(8,128)(2,1)S(1)}, u32[]{:S(2)}) copy-start(bf16[1,128,256]{1,2,0:T(8,128)(2,1)S(1)} %copy.267) | copy-start | bytes 196612
  34.4 1.7 %copy-start.18 = (bf16[1,384,256]{1,2,0:T(8,128)(2,1)}, bf16[1,384,256]{1,2,0:T(8,128)(2,1)S(1)}, u32[]{:S(2)}) copy-start(bf16[1,384,256]{1,2,0:T(8,128)(2,1)S(1)} %get-tuple-element.113) | copy-start | bytes 589828
  34.4 7.2 %copy-start.16 = (bf16[1,384,256]{1,2,0:T(8,128)(2,1)}, bf16[1,384,256]{1,2,0:T(8,128)(2,1)S(1)}, u32[]{:S(2)}) copy-start(bf16[1,384,256]{1,2,0:T(8,128)(2,1)S(1)} %get-tuple-element.110) | copy-start | bytes 589828
  34.4 13.4 %copy-start.14 = (bf16[1,384,256]{1,2,0:T(8,128)(2,1)}, bf16[1,384,256]{1,2,0:T(8,128)(2,1)S(1)}, u32[]{:S(2)}) copy-start(bf16[1,384,256]{1,2,0:T(8,128)(2,1)S(1)} %get-tuple-element.111) | copy-start | bytes 589828
  34.4 19.0 %copy-start.12 = (bf16[1,384,256]{1,2,0:T(8,128)(2,1)}, bf16[1,384,256]{1,2,0:T(8,128)(2,1)S(1)}, u32[]{:S(2)}) copy-start(bf16[1,384,256]{1,2,0:T(8,128)(2,1)S(1)} %get-tuple-element.112) | copy-start | bytes 589828
  38.7 0.8 copy-start.32
  38.7 1.1 %copy-start.30 = (bf16[1,128,256]{1,2,0:T(8,128)(2,1)S(1)}, bf16[1,128,256]{1,2,0:T(8,128)(2,1)}, u32[]{:S(2)}) copy-start(bf16[1,128,256]{1,2,0:T(8,128)(2,1)} %copy.347) | copy-start | bytes 196612
  38.7 1.1 %copy-start.46 = (pred[128,384]{0,1:T(8,128)(4,1)S(1)}, pred[128,384]{0,1:T(8,128)(4,1)}, u32[]{:S(2)}) copy-start(pred[128,384]{0,1:T(8,128)(4,1)} %copy-done.45) | copy-start | bytes 147460
  40.3 1.2 %copy-start.43 = (bf16[1,128,256]{1,2,0:T(8,128)(2,1)S(1)}, bf16[1,128,256]{1,2,0:T(8,128)(2,1)}, u32[]{:S(2)}) copy-start(bf16[1,128,256]{1,2,0:T(8,128)(2,1)} %copy.273) | copy-start | bytes 196612
  43.4 0.7 copy-start
  44.1 1.6 %copy-start.34 = (bf16[1,384,256]{1,2,0:T(8,128)(2,1)S(1)}, bf16[1,384,256]{1,2,0:T(8,128)(2,1)}, u32[]{:S(2)}) copy-start(bf16[1,384,256]{1,2,0:T(8,128)(2,1)} %get-tuple-element.71) | copy-start | bytes 589828
  45.7 2.1 %copy-start.42 = (bf16[1,128,256]{1,2,0:T(8,128)(2,1)S(1)}, bf16[1,128,256]{1,2,0:T(8,128)(2,1)}, u32[]{:S(2)}) copy-start(bf16[1,128,256]{1,2,0:T(8,128)(2,1)} %copy.279) | copy-start | bytes 196612
  50.3 1.2 %copy-start.47 = (pred[128,384]{0,1:T(8,128)(4,1)S(1)}, pred[128,384]{0,1:T(8,128)(4,1)}, u32[]{:S(2)}) copy-start(pred[128,384]{0,1:T(8,128)(4,1)} %copy-done.45) | copy-start | bytes 147460
  50.4 0.8 copy-start.2
  51.2 0.9 copy-start.33
  52.1 1.2 %copy-start.41 = (bf16[1,128,256]{1,2,0:T(8,128)(2,1)S(1)}, bf16[1,128,256]{1,2,0:T(8,128)(2,1)}, u32[]{:S(2)}) copy-start(bf16[1,128,256]{1,2,0:T(8,128)(2,1)} %copy.285) | copy-start | bytes 196612
  55.5 1.0 %copy-start.22 = (f32[4,64,384]{2,1,0:T(8,128)S(1)}, f32[4,64,384]{2,1,0:T(8,128)}, u32[]{:S(2)}) copy-start(f32[4,64,384]{2,1,0:T(8,128)} %fusion.60) | copy-start | bytes 1179652
  55.5 1.1 %copy-start.23 = (f32[4,64,384]{2,1,0:T(8,128)S(1)}, f32[4,64,384]{2,1,0:T(8,128)}, u32[]{:S(2)}) copy-start(f32[4,64,384]{2,1,0:T(8,128)} %fusion.57) | copy-start | bytes 1179652
  55.5 1.2 %copy-start.24 = (f32[4,64,384]{2,1,0:T(8,128)S(1)}, f32[4,64,384]{2,1,0:T(8,128)}, u32[]{:S(2)}) copy-start(f32[4,64,384]{2,1,0:T(8,128)} %fusion.54) | copy-start | bytes 1179652
  55.5 1.3 %copy-start.25 = (f32[4,64,384]{2,1,0:T(8,128)S(1)}, f32[4,64,384]{2,1,0:T(8,128)}, u32[]{:S(2)}) copy-start(f32[4,64,384]{2,1,0:T(8,128)} %fusion.51) | copy-start | bytes 1179652
  57.1 0.9 copy-start.19
  57.1 1.8 %copy-start.1 = (bf16[4,128,384]{1,2,0:T(8,128)(2,1)S(1)}, bf16[4,128,384]{1,2,0:T(8,128)(2,1)}, u32[]{:S(2)}) copy-start(bf16[4,128,384]{1,2,0:T(8,128)(2,1)} %copy-done) | copy-start | bytes 1179652
  57.1 1.8 %copy-start.17 = (bf16[1,384,256]{1,2,0:T(8,128)(2,1)S(1)}, bf16[1,384,256]{1,2,0:T(8,128)(2,1)}, u32[]{:S(2)}) copy-start(bf16[1,384,256]{1,2,0:T(8,128)(2,1)} %copy-done.16) | copy-start | bytes 589828
  57.1 2.6 %copy-start.3 = (bf16[4,128,384]{1,2,0:T(8,128)(2,1)S(1)}, bf16[4,128,384]{1,2,0:T(8,128)(2,1)}, u32[]{:S(2)}) copy-start(bf16[4,128,384]{1,2,0:T(8,128)(2,1)} %copy-done.2) | copy-start | bytes 1179652
  57.1 2.6 %copy-start.15 = (bf16[1,384,256]{1,2,0:T(8,128)(2,1)S(1)}, bf16[1,384,256]{1,2,0:T(8,128)(2,1)}, u32[]{:S(2)}) copy-start(bf16[1,384,256]{1,2,0:T(8,128)(2,1)} %copy-done.14) | copy-start | bytes 589828
  58.0 2.6 %copy-start.37 = (bf16[1,128,4,64]{1,3,2,0:T(8,128)(2,1)S(1)}, bf16[1,128,4,64]{1,3,2,0:T(8,128)(2,1)}, u32[]{:S(2)}) copy-start(bf16[1,128,4,64]{1,3,2,0:T(8,128)(2,1)} %fusion.37) | copy-start | bytes 196612
  58.0 2.9 %copy-start.38 = (bf16[1,128,4,64]{1,3,2,0:T(8,128)(2,1)S(1)}, bf16[1,128,4,64]{1,3,2,0:T(8,128)(2,1)}, u32[]{:S(2)}) copy-start(bf16[1,128,4,64]{1,3,2,0:T(8,128)(2,1)} %fusion.38) | copy-start | bytes 196612
  58.9 2.3 %copy-start.39 = (bf16[1,128,4,64]{1,3,2,0:T(8,128)(2,1)S(1)}, bf16[1,128,4,64]{1,3,2,0:T(8,128)(2,1)}, u32[]{:S(2)}) copy-start(bf16[1,128,4,64]{1,3,2,0:T(8,128)(2,1)} %fusion.39) | copy-start | bytes 196612
  58.9 2.6 %copy-start.40 = (bf16[1,128,4,64]{1,3,2,0:T(8,128)(2,1)S(1)}, bf16[1,128,4,64]{1,3,2,0:T(8,128)(2,1)}, u32[]{:S(2)}) copy-start(bf16[1,128,4,64]{1,3,2,0:T(8,128)(2,1)} %fusion.40) | copy-start | bytes 196612
  62.6 21.0 %all-to-all-start.1 = ((bf16[1,32,4,1024]{3,2,0,1:T(4,128)(2,1)}), bf16[1,32,4,1024]{3,2,0,1:T(4,128)(2,1)}, u32[]{:S(2)}, u32[]{:S(2)}) async-start(bf16[1,32,4,1024]{3,2,0,1:T(4,128)(2,1)} %maximum_bitcast_fusion.2), calls=%async_computation.1 | async-start | bytes 524288 | tf_op jit(solution)/shard_map/all_to_all | solution.py:126
  73.5 6.1 %copy-start.28 = (bf16[1,128,4,64]{1,3,2,0:T(8,128)(2,1)S(1)}, bf16[1,128,4,64]{1,3,2,0:T(8,128)(2,1)}, u32[]{:S(2)}) copy-start(bf16[1,128,4,64]{1,3,2,0:T(8,128)(2,1)} %fusion.36) | copy-start | bytes 196612
  74.5 16.6 %collective-permute-start.2 = (bf16[2,1,32,4,1024]{4,3,2,1,0:T(4,128)(2,1)}, bf16[2,1,32,4,1024]{4,3,2,1,0:T(4,128)(2,1)}, u32[]{:S(2)}, u32[]{:S(2)}) collective-permute-start(bf16[2,1,32,4,1024]{4,3,2,1,0:T(4,128)(2,1)} %convert_element_type.190), channel_id=1, source_target_pairs={{248,0},{0,8},{8,16},{16,24},{24,32},{32,40},{40,48},{48,56},{56,6... | collective-permute-start | bytes 1572872 | tf_op jit(solution)/shard_map/ppermute | solution.py:32
  74.7 7.6 %copy-start.13 = (bf16[1,384,256]{1,2,0:T(8,128)(2,1)S(1)}, bf16[1,384,256]{1,2,0:T(8,128)(2,1)}, u32[]{:S(2)}) copy-start(bf16[1,384,256]{1,2,0:T(8,128)(2,1)} %copy-done.12) | copy-start | bytes 589828
  75.7 15.4 %collective-permute-start.3 = (bf16[2,1,32,4,1024]{4,3,2,1,0:T(4,128)(2,1)}, bf16[2,1,32,4,1024]{4,3,2,1,0:T(4,128)(2,1)}, u32[]{:S(2)}, u32[]{:S(2)}) collective-permute-start(bf16[2,1,32,4,1024]{4,3,2,1,0:T(4,128)(2,1)} %convert_element_type.192), channel_id=1, source_target_pairs={{8,0},{16,8},{24,16},{32,24},{40,32},{48,40},{56,48},{64,56},{72,6... | collective-permute-start | bytes 1572872 | tf_op jit(solution)/shard_map/ppermute | solution.py:32
  79.8 5.1 %copy-start.11 = (f32[16,16,8,8]{2,3,1,0:T(8,128)S(1)}, f32[16,16,8,8]{2,3,1,0:T(8,128)}, u32[]{:S(2)}) copy-start(f32[16,16,8,8]{2,3,1,0:T(8,128)} %copy-done.10) | copy-start | bytes 196612
  79.8 5.1 %copy-start.21 = (bf16[8,16,16,64]{3,2,1,0:T(8,128)(2,1)S(1)}, bf16[8,16,16,64]{3,2,1,0:T(8,128)(2,1)}, u32[]{:S(2)}) copy-start(bf16[8,16,16,64]{3,2,1,0:T(8,128)(2,1)} %copy-done.20) | copy-start | bytes 786436
  84.9 1.9 %copy-start.36 = (f32[16,16,8]{2,1,0:T(8,128)S(1)}, f32[16,16,8]{2,1,0:T(8,128)}, u32[]{:S(2)}) copy-start(f32[16,16,8]{2,1,0:T(8,128)} %copy-done.35) | copy-start | bytes 24580
  86.8 1.0 %copy-start.7 = (bf16[8,16,16,64]{3,2,1,0:T(8,128)(2,1)S(1)}, bf16[8,16,16,64]{3,2,1,0:T(8,128)(2,1)}, u32[]{:S(2)}) copy-start(bf16[8,16,16,64]{3,2,1,0:T(8,128)(2,1)} %copy-done.6) | copy-start | bytes 786436
  87.9 1.6 %copy-start.5 = (bf16[8,16,16,64]{3,2,1,0:T(8,128)(2,1)S(1)}, bf16[8,16,16,64]{3,2,1,0:T(8,128)(2,1)}, u32[]{:S(2)}) copy-start(bf16[8,16,16,64]{3,2,1,0:T(8,128)(2,1)} %copy-done.4) | copy-start | bytes 786436
where the time goes:
time: 94.6 us; the launch traced here: 93.6 us
  local copies, waits for them, and re-layouts  34.2 us (36%)
  matrix products  25.4 us (27%)
  starting transfers between devices  23.2 us (25%)
  other arithmetic  6.55 us (7%)
  waiting for transfers between devices  2.68 us (3%)
  between operations  1.56 us (2%)
    unnamed x106, local copies, waits for them, and re-layouts  8.48 us
    all_to_all x1, starting transfers between devices, on_device(): lax.all_to_all(grad_col, 'lev', split_axis=0, concat_axis=1, tiled=True)  7.17 us
    ppermute x1, starting transfers between devices, padded(): after = lax.ppermute(first, axis, down)  6.38 us
    dot_general x4, matrix products, on_device(): jnp.einsum('lhqk,lqhd->lkhd', probs_b, grad_part, preferred_element_type=...  6.35 us
    dot_general x4, matrix products, on_device(): jnp.einsum('lhqk,lkhd->lqhd', attn_probs.astype(jnp.bfloat16), attend_val...  5.77 us
    all_to_all x1, starting transfers between devices, on_device(): lax.all_to_all(attended, 'lev', split_axis=1, concat_axis=0, tiled=True)  5.71 us
    ppermute x2, starting transfers between devices, from_behind(): return lax.ppermute(block, axis, route)  3.85 us
    reshape x4, local copies, waits for them, and re-layouts, column_heads(): return array.reshape(column_levels, lat_col * lon_dev, HEADS, head_dim)  3.34 us
  transfers between devices with their start and end apart: 6, of which 1 were waited for; matrix products, arithmetic and copies ran while one was open for 32% of the time, Pallas kernels for 0%

commit v1 on v0

v1 whole, which is shorter than its diff:
```python
import functools
import math

import jax
import jax.numpy as jnp
from jax import lax
from jax.experimental import pallas as pl
from jax.experimental.pallas import tpu as pltpu
from jax.sharding import PartitionSpec as P

HEADS = 16
HALO = 4
ROWS = 128
PAIR = 128
NEGATIVE = -1e30
F32 = jnp.float32
BF16 = jnp.bfloat16

VMEM = pl.BlockSpec(memory_space=pltpu.VMEM)
SMEM = pl.BlockSpec(memory_space=pltpu.SMEM)


def tokens(ref, pair):
    return ref[:, :, :, pl.ds(pair * PAIR, PAIR)].reshape(ROWS, PAIR)


def put(ref, pair, value):
    shape = ref.shape[:-1] + (PAIR,)
    ref[:, :, :, pl.ds(pair * PAIR, PAIR)] = value.astype(ref.dtype).reshape(shape)


def both_heads(block):
    lane = lax.broadcasted_iota(jnp.int32, (1, PAIR), 1)
    first = (lane < PAIR // 2).astype(F32).astype(BF16)
    second = (lane >= PAIR // 2).astype(F32).astype(BF16)
    return jnp.concatenate([block * first, block * second], axis=0)


def outer(a, b):
    return lax.dot_general(a, b, (((1,), (1,)), ((), ())), preferred_element_type=F32)


def inner(a, b):
    return lax.dot_general(a, b, (((1,), (0,)), ((), ())), preferred_element_type=F32)


def own_features(both):
    half = PAIR // 2
    return jnp.concatenate([both[:half, :ROWS], both[half:, ROWS:]], axis=0)


def softmax_over_rows(scores):
    top = jnp.max(scores, axis=0, keepdims=True)
    raised = jnp.exp(scores - top)
    return raised * (1.0 / jnp.sum(raised, axis=0, keepdims=True))


def score_grads(probs, d_probs):
    return probs * (d_probs - jnp.sum(probs * d_probs, axis=0, keepdims=True))


def column_bias():
    key = lax.broadcasted_iota(jnp.int32, (ROWS, 2 * ROWS), 0)
    query = lax.broadcasted_iota(jnp.int32, (ROWS, 2 * ROWS), 1)
    return jnp.where((key & 15) == (query & 15), 0.0, NEGATIVE).astype(F32)


def column_forward(q_ref, k_ref, g_ref, out_ref):
    bias = column_bias()
    for pair in range(HEADS // 2):
        queries = both_heads(tokens(q_ref, pair) * BF16(0.125))
        probs = softmax_over_rows(outer(tokens(k_ref, pair), queries) + bias)
        put(out_ref, pair, inner(probs.astype(BF16), both_heads(tokens(g_ref, pair))))


def column_backward(q_ref, k_ref, g_ref, a_ref, dq_ref, dk_ref):
    bias = column_bias()
    for pair in range(HEADS // 2):
        queries = both_heads(tokens(q_ref, pair) * BF16(0.125))
        keys = tokens(k_ref, pair)
        probs = softmax_over_rows(outer(keys, queries) + bias)
        d_probs = outer(tokens(a_ref, pair), both_heads(tokens(g_ref, pair)))
        d_scores = score_grads(probs, d_probs).astype(BF16)
        put(dk_ref, pair, inner(d_scores, queries))
        grad_query = own_features(inner(keys.T, d_scores)) * 0.125
        put(dq_ref, pair, grad_query.astype(BF16).T)


def level_bias(lists_ref):
    lane = lax.broadcasted_iota(jnp.int32, (1, ROWS), 1)
    listed = jnp.zeros((1, ROWS), jnp.int32)
    for block in range(4):
        bits = jnp.int32(0)
        for j in range(15):
            bits = bits | lax.shift_left(jnp.int32(1), lists_ref[0, block, j])
        listed = jnp.where(lane // 32 == block, bits, listed)
    row = lax.broadcasted_iota(jnp.int32, (3 * ROWS, ROWS), 0)
    part = row // ROWS
    lat = (row % ROWS) // 4
    column = row % 4
    key_block = (lat // 8) * 6 + part * 2 + column // 2
    allowed = lax.shift_right_logical(jnp.broadcast_to(listed, row.shape), key_block) & 1
    return jnp.where(allowed == 1, 0.0, NEGATIVE).astype(F32)


def level_kernel(
    lists_ref, q_ref, k_ref, v_ref, kl_ref, vl_ref, kr_ref, vr_ref, g_ref,
    att_ref, dq_ref, dk_ref, dv_ref, dkl_ref, dvl_ref, dkr_ref, dvr_ref,
):
    bias = level_bias(lists_ref)
    bias = jnp.concatenate([bias, bias], axis=1)
    for pair in range(HEADS // 2):
        queries = both_heads(tokens(q_ref, pair) * BF16(0.125))
        grads = both_heads(tokens(g_ref, pair))
        keys = jnp.concatenate([tokens(r, pair) for r in (kl_ref, k_ref, kr_ref)], axis=0)
        values = jnp.concatenate([tokens(r, pair) for r in (vl_ref, v_ref, vr_ref)], axis=0)
        probs = softmax_over_rows(outer(keys, queries) + bias)
        probs_b = probs.astype(BF16)
        attended = own_features(inner(values.T, probs_b))
        put(att_ref, pair, attended.astype(BF16).T)
        d_scores = score_grads(probs, outer(values, grads)).astype(BF16)
        grad_query = own_features(inner(keys.T, d_scores)) * 0.125
        put(dq_ref, pair, grad_query.astype(BF16).T)
        key_terms = inner(d_scores, queries)
        value_terms = inner(probs_b, grads)
        for ref, at in ((dkl_ref, 0), (dk_ref, 1), (dkr_ref, 2)):
            put(ref, pair, key_terms[at * ROWS : (at + 1) * ROWS])
        for ref, at in ((dvl_ref, 0), (dv_ref, 1), (dvr_ref, 2)):
            put(ref, pair, value_terms[at * ROWS : (at + 1) * ROWS])


def sum_kernel(dk_ref, dv_ref, kl_ref, vl_ref, kr_ref, vr_ref, gk_ref, gv_ref):
    gk_ref[...] = (dk_ref[...] + kl_ref[...].astype(F32) + kr_ref[...].astype(F32)).astype(BF16)
    gv_ref[...] = (dv_ref[...] + vl_ref[...].astype(F32) + vr_ref[...].astype(F32)).astype(BF16)


def call(kernel, outs, args, flops, smem=0):
    moved = sum(a.size * a.dtype.itemsize for a in args)
    return pl.pallas_call(
        kernel,
        out_shape=outs,
        in_specs=[SMEM] * smem + [VMEM] * (len(args) - smem),
        out_specs=[VMEM] * len(outs),
        cost_estimate=pl.CostEstimate(flops=flops, bytes_accessed=moved, transcendentals=0),
        compiler_params=pltpu.CompilerParams(vmem_limit_bytes=40 * 2**20),
    )(*args)


def on_device(
    query_level, key_level, value_level, block_lists, query_column, key_column, grad_output
):
    size = lax.axis_size("lon")
    up = [(i, (i + 1) % size) for i in range(size)]
    down = [(j, i) for i, j in up]
    level = jax.ShapeDtypeStruct(query_level.shape, BF16)
    level32 = jax.ShapeDtypeStruct(query_level.shape, F32)
    column = jax.ShapeDtypeStruct(query_column.shape, BF16)
    key_left = lax.ppermute(key_level, "lon", up)
    key_right = lax.ppermute(key_level, "lon", down)
    value_left = lax.ppermute(value_level, "lon", up)
    value_right = lax.ppermute(value_level, "lon", down)
    unit = 2 * ROWS * ROWS * 1024
    (grad_col,) = call(
        column_forward, [column], [query_column, key_column, grad_output], 4 * unit
    )
    grad_att = lax.all_to_all(grad_col, "lev", split_axis=0, concat_axis=1, tiled=True)
    attended, grad_query, dk, dv, dkl, dvl, dkr, dvr = call(
        level_kernel,
        [level, level, level32, level32, level, level, level, level],
        [block_lists, query_level, key_level, value_level,
         key_left, value_left, key_right, value_right, grad_att],
        18 * unit,
        smem=1,
    )
    columns = lax.all_to_all(attended, "lev", split_axis=1, concat_axis=0, tiled=True)
    key_from_right = lax.ppermute(dkl, "lon", down)
    key_from_left = lax.ppermute(dkr, "lon", up)
    value_from_right = lax.ppermute(dvl, "lon", down)
    value_from_left = lax.ppermute(dvr, "lon", up)
    grad_query_column, grad_key_column = call(
        column_backward, [column, column], [query_column, key_column, grad_output, columns],
        6 * unit,
    )
    grad_key, grad_value = call(
        sum_kernel, [level, level],
        [dk, dv, key_from_left, value_from_left, key_from_right, value_from_right],
        unit,
    )
    return grad_query, grad_key, grad_value, grad_query_column, grad_key_column


def solution(mesh):
    level = P("lev", None, "lon", None)
    column = P(None, "lev", "lon", None)
    return jax.shard_map(
        on_device,
        mesh=mesh,
        in_specs=(level, level, level, P("lon", None, None), column, column, column),
        out_specs=(level, level, level, column, column),
        check_vma=False,
    )
```

time: 94.6 us -> 58.5 us (0.62)
  the two profiles are of different devices: /device:TPU:2 before, /device:TPU:1 now
where the time goes in v1:
time: 58.5 us; the launch traced here: 58.3 us
  blocking collectives  23.7 us (41%)
  starting transfers between devices  17.2 us (29%)
  Pallas kernels  13.7 us (23%)
  local copies, waits for them, and re-layouts  2.88 us (5%)
  between operations  0.73 us (1%)
    pallas_call x4, Pallas kernels, call(): pl.pallas_call(kernel, out_shape=outs, in_specs=[SMEM] * smem + [VMEM] *...  13.7 us
    all_to_all x1, blocking collectives, on_device(): lax.all_to_all(grad_col, 'lev', split_axis=0, concat_axis=1, tiled=True)  13.6 us
    all_to_all x1, blocking collectives, on_device(): lax.all_to_all(attended, 'lev', split_axis=1, concat_axis=0, tiled=True)  10.2 us
    ppermute x1, starting transfers between devices, on_device(): key_from_right = lax.ppermute(dkl, 'lon', down)  4.47 us
    ppermute x1, starting transfers between devices, on_device(): value_from_right = lax.ppermute(dvl, 'lon', down)  3.88 us
    ppermute x1, starting transfers between devices, on_device(): value_right = lax.ppermute(value_level, 'lon', down)  3.13 us
    ppermute x1, starting transfers between devices, on_device(): key_left = lax.ppermute(key_level, 'lon', up)  3.1 us
    unnamed x20, local copies, waits for them, and re-layouts  2.88 us
  transfers between devices with their start and end apart: 8, of which 0 were waited for; matrix products, arithmetic and copies ran while one was open for 0% of the time, Pallas kernels for 7%

profile of v1, /device:TPU:1, one launch (start us, length us, event | category | flops | bytes accessed | tf_op | source)
XLA Modules:
  0.0 58.3 jit_solution(11152613600157929199)
XLA Ops:
  0.6 3.1 %collective-permute-start = (bf16[1,32,4,1024]{3,2,1,0:T(4,128)(2,1)}, bf16[1,32,4,1024]{3,2,1,0:T(4,128)(2,1)S(1)}, u32[]{:S(2)}, u32[]{:S(2)}) collective-permute-start(bf16[1,32,4,1024]{3,2,1,0:T(4,128)(2,1)} %k_ref.4), channel_id=1, source_target_pairs={{0,8},{8,16},{16,24},{24,32},{32,40},{40,48},{48,56},{56,64},{64,7... | collective-permute-start | bytes 786440 | tf_op jit(solution)/shard_map/ppermute | solution.py:158
  3.7 0.3 collective-permute-start.2
  4.0 1.4 %collective-permute-start.1 = (bf16[1,32,4,1024]{3,2,1,0:T(4,128)(2,1)}, bf16[1,32,4,1024]{3,2,1,0:T(4,128)(2,1)S(1)}, u32[]{:S(2)}, u32[]{:S(2)}) collective-permute-start(bf16[1,32,4,1024]{3,2,1,0:T(4,128)(2,1)} %v_ref.1), channel_id=1, source_target_pairs={{0,8},{8,16},{16,24},{24,32},{32,40},{40,48},{48,56},{56,64},{64,7... | collective-permute-start | bytes 786440 | tf_op jit(solution)/shard_map/ppermute | solution.py:160
  5.5 3.1 %collective-permute-start.3 = (bf16[1,32,4,1024]{3,2,1,0:T(4,128)(2,1)}, bf16[1,32,4,1024]{3,2,1,0:T(4,128)(2,1)S(1)}, u32[]{:S(2)}, u32[]{:S(2)}) collective-permute-start(bf16[1,32,4,1024]{3,2,1,0:T(4,128)(2,1)} %v_ref.1), channel_id=1, source_target_pairs={{8,0},{16,8},{24,16},{32,24},{40,32},{48,40},{56,48},{64,56},{72,6... | collective-permute-start | bytes 786440 | tf_op jit(solution)/shard_map/ppermute | solution.py:161
  8.6 0.0 copy-start
  8.6 0.9 %copy-done = bf16[8,4,4,1024]{3,2,1,0:T(4,128)(2,1)S(1)} copy-done((bf16[8,4,4,1024]{3,2,1,0:T(4,128)(2,1)S(1)}, bf16[8,4,4,1024]{3,2,1,0:T(4,128)(2,1)}, u32[]{:S(2)}) %copy-start) | copy-done | bytes 262168
  9.6 0.0 copy-start.2
  9.6 0.9 %copy-done.2 = bf16[8,4,4,1024]{3,2,1,0:T(4,128)(2,1)S(1)} copy-done((bf16[8,4,4,1024]{3,2,1,0:T(4,128)(2,1)S(1)}, bf16[8,4,4,1024]{3,2,1,0:T(4,128)(2,1)}, u32[]{:S(2)}) %copy-start.2) | copy-done | bytes 262168
  10.5 0.0 copy-start.4
  10.5 0.9 %copy-done.4 = bf16[8,4,4,1024]{3,2,1,0:T(4,128)(2,1)S(1)} copy-done((bf16[8,4,4,1024]{3,2,1,0:T(4,128)(2,1)S(1)}, bf16[8,4,4,1024]{3,2,1,0:T(4,128)(2,1)}, u32[]{:S(2)}) %copy-start.4) | copy-done | bytes 262168
  11.5 0.0 copy-start.8
  11.5 0.0 copy-start.9
  11.5 1.0 %shard_map.110 = bf16[8,4,4,1024]{3,2,1,0:T(4,128)(2,1)S(1)} custom-call(bf16[8,4,4,1024]{3,2,1,0:T(4,128)(2,1)S(1)} %copy-done, bf16[8,4,4,1024]{3,2,1,0:T(4,128)(2,1)S(1)} %copy-done.2, bf16[8,4,4,1024]{3,2,1,0:T(4,128)(2,1)S(1)} %copy-done.4), custom_call_target="tpu_custom_call" | custom-call | flops 134217728 | bytes 786432 | tf_op jit(solution)/shard_map/pallas_call | solution.py:139
  12.5 0.0 copy-start.6
  12.5 0.0 copy-start.7
  12.5 13.6 %all_to_all.24 = bf16[8,4,4,1024]{3,2,1,0:T(4,128)(2,1)S(1)} all-to-all(bf16[8,4,4,1024]{3,2,1,0:T(4,128)(2,1)S(1)} %shard_map.110), channel_id=1, replica_groups=mesh['lon'=32,'lev'=8] {'lev'}, dimensions={0} | all-to-all | bytes 524288 | tf_op jit(solution)/shard_map/all_to_all | solution.py:166
  26.1 0.0 collective-permute-done.kl_ref
  26.1 0.0 collective-permute-done.2.kr_ref
  26.1 0.0 collective-permute-done.1.vl_ref
  26.1 0.0 collective-permute-done.3.vr_ref
  26.1 0.0 copy-done.8
  26.1 0.0 copy-done.9
  26.1 0.0 copy-done.6
  26.1 0.0 copy-done.7
  26.1 0.0 copy-start.5
  26.2 8.6 %shard_map.111 = (bf16[1,32,4,1024]{3,2,1,0:T(4,128)(2,1)S(1)}, bf16[1,32,4,1024]{3,2,1,0:T(4,128)(2,1)}, f32[1,32,4,1024]{3,2,1,0:T(4,128)S(1)}, f32[1,32,4,102...) custom-call(s32[1,4,15]{2,1,0:T(4,128)S(1)} %copy-done.9, ...), custom_call_target="tpu_custom_call" | custom-call | flops 603979776 | bytes 2097392 | tf_op jit(solution)/shard_map/pallas_call | solution.py:139
  34.7 0.8 %collective-permute-start.4 = (bf16[1,32,4,1024]{3,2,1,0:T(4,128)(2,1)S(1)}, bf16[1,32,4,1024]{3,2,1,0:T(4,128)(2,1)S(1)}, u32[]{:S(2)}, u32[]{:S(2)}) collective-permute-start(bf16[1,32,4,1024]{3,2,1,0:T(4,128)(2,1)S(1)} %get-tuple-element.20), channel_id=1, source_target_pairs={{0,8},{8,16},{16,24},{24,32},{32,40},{40,48},{48,56},{56,64},{64,7... | collective-permute-start | bytes 786440 | tf_op jit(solution)/shard_map/ppermute | solution.py:177
  35.5 0.0 collective-permute-start.5
  35.5 4.5 %collective-permute-start.6 = (bf16[1,32,4,1024]{3,2,1,0:T(4,128)(2,1)S(1)}, bf16[1,32,4,1024]{3,2,1,0:T(4,128)(2,1)S(1)}, u32[]{:S(2)}, u32[]{:S(2)}) collective-permute-start(bf16[1,32,4,1024]{3,2,1,0:T(4,128)(2,1)S(1)} %get-tuple-element.22), channel_id=1, source_target_pairs={{8,0},{16,8},{24,16},{32,24},{40,32},{48,40},{56,48},{64,56},{72,6... | collective-permute-start | bytes 786440 | tf_op jit(solution)/shard_map/ppermute | solution.py:176
  40.0 3.9 %collective-permute-start.7 = (bf16[1,32,4,1024]{3,2,1,0:T(4,128)(2,1)S(1)}, bf16[1,32,4,1024]{3,2,1,0:T(4,128)(2,1)S(1)}, u32[]{:S(2)}, u32[]{:S(2)}) collective-permute-start(bf16[1,32,4,1024]{3,2,1,0:T(4,128)(2,1)S(1)} %get-tuple-element.23), channel_id=1, source_target_pairs={{8,0},{16,8},{24,16},{32,24},{40,32},{48,40},{56,48},{64,56},{72,6... | collective-permute-start | bytes 786440 | tf_op jit(solution)/shard_map/ppermute | solution.py:178
  43.9 0.0 copy-start.1
  43.9 0.0 copy-start.3
  43.9 10.2 %all_to_all.25 = bf16[1,32,4,1024]{3,2,0,1:T(4,128)(2,1)S(1)} all-to-all(bf16[1,32,4,1024]{3,2,0,1:T(4,128)(2,1)S(1)} %bitcast.4), channel_id=1, replica_groups=mesh['lon'=32,'lev'=8] {'lev'}, dimensions={1} | all-to-all | bytes 524288 | tf_op jit(solution)/shard_map/all_to_all | solution.py:175
  54.1 0.0 copy-done.5
  54.1 0.0 copy-done.1
  54.1 0.0 copy-done.3
  54.1 3.2 %shard_map.113 = (bf16[8,4,4,1024]{3,2,1,0:T(4,128)(2,1)}, bf16[8,4,4,1024]{3,2,1,0:T(4,128)(2,1)}) custom-call(bf16[8,4,4,1024]{3,2,1,0:T(4,128)(2,1)S(1)} %copy-done.1, bf16[8,4,4,1024]{3,2,1,0:T(4,128)(2,1)S(1)} %copy-done.3, bf16[8,4,4,1024]{3,2,1,0:T(4,128)(2,1)S(1)} %copy-done.5, bf16[8,4,4,1024]{3,2,1,0:T(4,128)(2,1)S(1)} %bitcast.3), custom_call_target="tpu_custom_call" | custom-call | flops 201326592 | bytes 1048576 | tf_op jit(solution)/shard_map/pallas_call | solution.py:139
  57.2 0.0 collective-permute-done.4.kl_ref
  57.2 0.0 collective-permute-done.5.vl_ref
  57.2 0.0 collective-permute-done.6.kr_ref
  57.2 0.0 collective-permute-done.7.vr_ref
  57.3 1.0 %shard_map.112 = (bf16[1,32,4,1024]{3,2,1,0:T(4,128)(2,1)}, bf16[1,32,4,1024]{3,2,1,0:T(4,128)(2,1)}) custom-call(f32[1,32,4,1024]{3,2,1,0:T(4,128)S(1)} %get-tuple-element.18.dk_ref, f32[1,32,4,1024]{3,2,1,0:T(4,128)S(1)} %get-tuple-element.19.dv_ref, bf16[1,32,4,1024]{3,2,1,0:T(4,128)(2,1)S(1)} %collective-permute-done.4.kl_ref, ...), custom_call_target="tpu_custom_call" | custom-call | flops 33554432 | bytes 2097152 | tf_op jit(solution)/shard_map/pallas_call | solution.py:139
Async XLA Ops:
  0.6 25.4 %collective-permute-start = (bf16[1,32,4,1024]{3,2,1,0:T(4,128)(2,1)}, bf16[1,32,4,1024]{3,2,1,0:T(4,128)(2,1)S(1)}, u32[]{:S(2)}, u32[]{:S(2)}) collective-permute-start(bf16[1,32,4,1024]{3,2,1,0:T(4,128)(2,1)} %k_ref.4), channel_id=1, source_target_pairs={{0,8},{8,16},{16,24},{24,32},{32,40},{40,48},{48,56},{56,64},{64,7... | collective-permute-start | bytes 786440 | tf_op jit(solution)/shard_map/ppermute | solution.py:158
  3.7 22.3 %collective-permute-start.2 = (bf16[1,32,4,1024]{3,2,1,0:T(4,128)(2,1)}, bf16[1,32,4,1024]{3,2,1,0:T(4,128)(2,1)S(1)}, u32[]{:S(2)}, u32[]{:S(2)}) collective-permute-start(bf16[1,32,4,1024]{3,2,1,0:T(4,128)(2,1)} %k_ref.4), channel_id=1, source_target_pairs={{8,0},{16,8},{24,16},{32,24},{40,32},{48,40},{56,48},{64,56},{72,6... | collective-permute-start | bytes 786440 | tf_op jit(solution)/shard_map/ppermute | solution.py:159
  4.0 22.0 %collective-permute-start.1 = (bf16[1,32,4,1024]{3,2,1,0:T(4,128)(2,1)}, bf16[1,32,4,1024]{3,2,1,0:T(4,128)(2,1)S(1)}, u32[]{:S(2)}, u32[]{:S(2)}) collective-permute-start(bf16[1,32,4,1024]{3,2,1,0:T(4,128)(2,1)} %v_ref.1), channel_id=1, source_target_pairs={{0,8},{8,16},{16,24},{24,32},{32,40},{40,48},{48,56},{56,64},{64,7... | collective-permute-start | bytes 786440 | tf_op jit(solution)/shard_map/ppermute | solution.py:160
  5.5 20.6 %collective-permute-start.3 = (bf16[1,32,4,1024]{3,2,1,0:T(4,128)(2,1)}, bf16[1,32,4,1024]{3,2,1,0:T(4,128)(2,1)S(1)}, u32[]{:S(2)}, u32[]{:S(2)}) collective-permute-start(bf16[1,32,4,1024]{3,2,1,0:T(4,128)(2,1)} %v_ref.1), channel_id=1, source_target_pairs={{8,0},{16,8},{24,16},{32,24},{40,32},{48,40},{56,48},{64,56},{72,6... | collective-permute-start | bytes 786440 | tf_op jit(solution)/shard_map/ppermute | solution.py:161
  8.6 0.9 %copy-start = (bf16[8,4,4,1024]{3,2,1,0:T(4,128)(2,1)S(1)}, bf16[8,4,4,1024]{3,2,1,0:T(4,128)(2,1)}, u32[]{:S(2)}) copy-start(bf16[8,4,4,1024]{3,2,1,0:T(4,128)(2,1)} %q_ref.5) | copy-start | bytes 786436
  9.6 0.9 %copy-start.2 = (bf16[8,4,4,1024]{3,2,1,0:T(4,128)(2,1)S(1)}, bf16[8,4,4,1024]{3,2,1,0:T(4,128)(2,1)}, u32[]{:S(2)}) copy-start(bf16[8,4,4,1024]{3,2,1,0:T(4,128)(2,1)} %k_ref.5) | copy-start | bytes 786436
  10.5 0.9 %copy-start.4 = (bf16[8,4,4,1024]{3,2,1,0:T(4,128)(2,1)S(1)}, bf16[8,4,4,1024]{3,2,1,0:T(4,128)(2,1)}, u32[]{:S(2)}) copy-start(bf16[8,4,4,1024]{3,2,1,0:T(4,128)(2,1)} %g_ref.3) | copy-start | bytes 786436
  11.5 14.6 %copy-start.8 = (bf16[1,32,4,1024]{3,2,1,0:T(4,128)(2,1)S(1)}, bf16[1,32,4,1024]{3,2,1,0:T(4,128)(2,1)}, u32[]{:S(2)}) copy-start(bf16[1,32,4,1024]{3,2,1,0:T(4,128)(2,1)} %v_ref.1) | copy-start | bytes 786436
  11.5 14.6 %copy-start.9 = (s32[1,4,15]{2,1,0:T(4,128)S(1)}, s32[1,4,15]{2,1,0:T(4,128)}, u32[]{:S(2)}) copy-start(s32[1,4,15]{2,1,0:T(4,128)} %lists_ref.1) | copy-start | bytes 724
  12.5 13.6 %copy-start.6 = (bf16[1,32,4,1024]{3,2,1,0:T(4,128)(2,1)S(1)}, bf16[1,32,4,1024]{3,2,1,0:T(4,128)(2,1)}, u32[]{:S(2)}) copy-start(bf16[1,32,4,1024]{3,2,1,0:T(4,128)(2,1)} %q_ref.4) | copy-start | bytes 786436
  12.5 13.6 %copy-start.7 = (bf16[1,32,4,1024]{3,2,1,0:T(4,128)(2,1)S(1)}, bf16[1,32,4,1024]{3,2,1,0:T(4,128)(2,1)}, u32[]{:S(2)}) copy-start(bf16[1,32,4,1024]{3,2,1,0:T(4,128)(2,1)} %k_ref.4) | copy-start | bytes 786436
  26.1 27.9 %copy-start.5 = (bf16[8,4,4,1024]{3,2,1,0:T(4,128)(2,1)S(1)}, bf16[8,4,4,1024]{3,2,1,0:T(4,128)(2,1)}, u32[]{:S(2)}) copy-start(bf16[8,4,4,1024]{3,2,1,0:T(4,128)(2,1)} %g_ref.3) | copy-start | bytes 786436
  34.7 22.5 %collective-permute-start.4 = (bf16[1,32,4,1024]{3,2,1,0:T(4,128)(2,1)S(1)}, bf16[1,32,4,1024]{3,2,1,0:T(4,128)(2,1)S(1)}, u32[]{:S(2)}, u32[]{:S(2)}) collective-permute-start(bf16[1,32,4,1024]{3,2,1,0:T(4,128)(2,1)S(1)} %get-tuple-element.20), channel_id=1, source_target_pairs={{0,8},{8,16},{16,24},{24,32},{32,40},{40,48},{48,56},{56,64},{64,7... | collective-permute-start | bytes 786440 | tf_op jit(solution)/shard_map/ppermute | solution.py:177
  35.5 21.7 %collective-permute-start.5 = (bf16[1,32,4,1024]{3,2,1,0:T(4,128)(2,1)S(1)}, bf16[1,32,4,1024]{3,2,1,0:T(4,128)(2,1)S(1)}, u32[]{:S(2)}, u32[]{:S(2)}) collective-permute-start(bf16[1,32,4,1024]{3,2,1,0:T(4,128)(2,1)S(1)} %get-tuple-element.21), channel_id=1, source_target_pairs={{0,8},{8,16},{16,24},{24,32},{32,40},{40,48},{48,56},{56,64},{64,7... | collective-permute-start | bytes 786440 | tf_op jit(solution)/shard_map/ppermute | solution.py:179
  35.5 21.7 %collective-permute-start.6 = (bf16[1,32,4,1024]{3,2,1,0:T(4,128)(2,1)S(1)}, bf16[1,32,4,1024]{3,2,1,0:T(4,128)(2,1)S(1)}, u32[]{:S(2)}, u32[]{:S(2)}) collective-permute-start(bf16[1,32,4,1024]{3,2,1,0:T(4,128)(2,1)S(1)} %get-tuple-element.22), channel_id=1, source_target_pairs={{8,0},{16,8},{24,16},{32,24},{40,32},{48,40},{56,48},{64,56},{72,6... | collective-permute-start | bytes 786440 | tf_op jit(solution)/shard_map/ppermute | solution.py:176
  40.0 17.2 %collective-permute-start.7 = (bf16[1,32,4,1024]{3,2,1,0:T(4,128)(2,1)S(1)}, bf16[1,32,4,1024]{3,2,1,0:T(4,128)(2,1)S(1)}, u32[]{:S(2)}, u32[]{:S(2)}) collective-permute-start(bf16[1,32,4,1024]{3,2,1,0:T(4,128)(2,1)S(1)} %get-tuple-element.23), channel_id=1, source_target_pairs={{8,0},{16,8},{24,16},{32,24},{40,32},{48,40},{56,48},{64,56},{72,6... | collective-permute-start | bytes 786440 | tf_op jit(solution)/shard_map/ppermute | solution.py:178
  43.9 10.2 %copy-start.1 = (bf16[8,4,4,1024]{3,2,1,0:T(4,128)(2,1)S(1)}, bf16[8,4,4,1024]{3,2,1,0:T(4,128)(2,1)}, u32[]{:S(2)}) copy-start(bf16[8,4,4,1024]{3,2,1,0:T(4,128)(2,1)} %q_ref.5) | copy-start | bytes 786436
  43.9 10.2 %copy-start.3 = (bf16[8,4,4,1024]{3,2,1,0:T(4,128)(2,1)S(1)}, bf16[8,4,4,1024]{3,2,1,0:T(4,128)(2,1)}, u32[]{:S(2)}) copy-start(bf16[8,4,4,1024]{3,2,1,0:T(4,128)(2,1)} %k_ref.5) | copy-start | bytes 786436

commit v2 on v1

v2 whole, which is shorter than its diff:
```python
import jax
import jax.numpy as jnp
from jax import lax
from jax.experimental import pallas as pl
from jax.experimental.pallas import tpu as pltpu
from jax.sharding import PartitionSpec as P

PAIRS = 8
ROWS = 128
PAIR = 128
NEGATIVE = -1e30
F32 = jnp.float32
BF16 = jnp.bfloat16

VMEM = pl.BlockSpec(memory_space=pltpu.VMEM)
SMEM = pl.BlockSpec(memory_space=pltpu.SMEM)
ANY = pl.BlockSpec(memory_space=pl.ANY)


def tokens(ref, pair):
    return ref[:, :, :, pl.ds(pair * PAIR, PAIR)].reshape(ROWS, PAIR)


def put(ref, pair, value):
    shape = ref.shape[:-1] + (PAIR,)
    ref[:, :, :, pl.ds(pair * PAIR, PAIR)] = value.astype(ref.dtype).reshape(shape)


def both_heads(block):
    lane = lax.broadcasted_iota(jnp.int32, (1, PAIR), 1)
    first = (lane < PAIR // 2).astype(F32).astype(BF16)
    second = (lane >= PAIR // 2).astype(F32).astype(BF16)
    return jnp.concatenate([block * first, block * second], axis=0)


def outer(a, b):
    return lax.dot_general(a, b, (((1,), (1,)), ((), ())), preferred_element_type=F32)


def inner(a, b):
    return lax.dot_general(a, b, (((1,), (0,)), ((), ())), preferred_element_type=F32)


def own_features(both):
    half = PAIR // 2
    return jnp.concatenate([both[:half, :ROWS], both[half:, ROWS:]], axis=0)


def softmax_over_rows(scores):
    top = jnp.max(scores, axis=0, keepdims=True)
    raised = jnp.exp(scores - top)
    return raised * (1.0 / jnp.sum(raised, axis=0, keepdims=True))


def score_grads(probs, d_probs):
    return probs * (d_probs - jnp.sum(probs * d_probs, axis=0, keepdims=True))


def column_bias():
    key = lax.broadcasted_iota(jnp.int32, (ROWS, 2 * ROWS), 0)
    query = lax.broadcasted_iota(jnp.int32, (ROWS, 2 * ROWS), 1)
    return jnp.where((key & 15) == (query & 15), 0.0, NEGATIVE).astype(F32)


def column_forward(
    q_hbm, k_hbm, g_hbm, lk_hbm, lv_hbm, lq_hbm, out_ref, both_ref, lq_ref, q_ref, k_ref, g_ref, sems
):
    moves = [
        (q_hbm, q_ref),
        (k_hbm, k_ref),
        (g_hbm, g_ref),
        (lk_hbm, both_ref.at[pl.ds(0, 1)]),
        (lv_hbm, both_ref.at[pl.ds(1, 1)]),
        (lq_hbm, lq_ref),
    ]
    copies = [
        pltpu.make_async_copy(src, dst, sems.at[i]) for i, (src, dst) in enumerate(moves)
    ]
    for copy in copies:
        copy.start()
    bias = column_bias()
    for copy in copies[:3]:
        copy.wait()
    for pair in range(PAIRS):
        queries = both_heads(tokens(q_ref, pair) * BF16(0.125))
        probs = softmax_over_rows(outer(tokens(k_ref, pair), queries) + bias)
        put(out_ref, pair, inner(probs.astype(BF16), both_heads(tokens(g_ref, pair))))
    for copy in copies[3:]:
        copy.wait()


def send(pair, moves, sems):
    lanes = pl.ds(pair * PAIR, PAIR)
    copies = [
        pltpu.make_async_copy(src.at[:, :, :, lanes], dst.at[:, :, :, lanes], sems.at[i, pair])
        for i, (src, dst) in enumerate(moves)
    ]
    for copy in copies:
        copy.start()
    return copies


def final_kernel(
    q_ref, k_ref, g_ref, a_ref, dk_ref, dv_ref, near_ref, far_ref,
    dq_hbm, dkc_hbm, gk_hbm, gv_hbm, dqc_ref, dkc_ref, gk_ref, gv_ref, sems,
):
    bias = column_bias()
    copies = []
    for pair in range(PAIRS):
        lanes = pl.ds(pair * PAIR, PAIR)
        queries = both_heads(tokens(q_ref, pair) * BF16(0.125))
        keys = tokens(k_ref, pair)
        probs = softmax_over_rows(outer(keys, queries) + bias)
        d_probs = outer(tokens(a_ref, pair), both_heads(tokens(g_ref, pair)))
        d_scores = score_grads(probs, d_probs).astype(BF16)
        put(dkc_ref, pair, inner(d_scores, queries))
        grad_query = own_features(inner(keys.T, d_scores)) * 0.125
        put(dqc_ref, pair, grad_query.astype(BF16).T)
        for at, (own, out) in enumerate(((dk_ref, gk_ref), (dv_ref, gv_ref))):
            rims = near_ref[pl.ds(at, 1), :, :, lanes].astype(F32) + far_ref[pl.ds(at, 1), :, :, lanes].astype(F32)
            out[:, :, :, lanes] = (own[:, :, :, lanes] + rims).astype(BF16)
        moves = [(dqc_ref, dq_hbm), (dkc_ref, dkc_hbm), (gk_ref, gk_hbm), (gv_ref, gv_hbm)]
        copies += send(pair, moves, sems)
    for copy in copies:
        copy.wait()


def level_bias(lists_ref):
    odd = lax.axis_index("lon") % 2
    lane = lax.broadcasted_iota(jnp.int32, (1, ROWS), 1)
    listed = jnp.zeros((1, ROWS), jnp.int32)
    for block in range(4):
        bits = jnp.int32(0)
        for j in range(15):
            bits = bits | lax.shift_left(jnp.int32(1), lists_ref[0, block, j])
        listed = jnp.where(lane // 32 == block, bits, listed)
    row = lax.broadcasted_iota(jnp.int32, (ROWS, ROWS), 0)
    block = (row // 32) * 6 + (row % 4) // 2
    parts = []
    for part in (2 - 2 * odd, 1, 2 * odd):
        allowed = lax.shift_right_logical(jnp.broadcast_to(listed, row.shape), block + 2 * part)
        parts.append(jnp.where((allowed & 1) == 1, 0.0, NEGATIVE).astype(F32))
    bias = jnp.concatenate(parts, axis=0)
    return jnp.concatenate([bias, bias], axis=1)


def halo(near, own, far, at, pair):
    return jnp.concatenate([tokens(r.at[pl.ds(at, 1)], pair) for r in (near, own, far)], axis=0)


def level_kernel(
    lists_ref, q_ref, both_ref, near_ref, far_ref, g_ref,
    dq_hbm, att_ref, dk_ref, dv_ref, near_out, far_out, dq_ref, sems,
):
    bias = level_bias(lists_ref)
    copies = []
    for pair in range(PAIRS):
        queries = both_heads(tokens(q_ref, pair) * BF16(0.125))
        grads = both_heads(tokens(g_ref, pair))
        keys = halo(near_ref, both_ref, far_ref, 0, pair)
        values = halo(near_ref, both_ref, far_ref, 1, pair)
        probs = softmax_over_rows(outer(keys, queries) + bias)
        probs_b = probs.astype(BF16)
        attended = own_features(inner(values.T, probs_b))
        put(att_ref, pair, attended.astype(BF16).T)
        d_scores = score_grads(probs, outer(values, grads)).astype(BF16)
        grad_query = own_features(inner(keys.T, d_scores)) * 0.125
        put(dq_ref, pair, grad_query.astype(BF16).T)
        copies += send(pair, [(dq_ref, dq_hbm)], sems)
        key_terms = inner(d_scores, queries)
        value_terms = inner(probs_b, grads)
        put(near_out.at[pl.ds(0, 1)], pair, key_terms[:ROWS])
        put(near_out.at[pl.ds(1, 1)], pair, value_terms[:ROWS])
        put(dk_ref, pair, key_terms[ROWS : 2 * ROWS])
        put(dv_ref, pair, value_terms[ROWS : 2 * ROWS])
        put(far_out.at[pl.ds(0, 1)], pair, key_terms[2 * ROWS :])
        put(far_out.at[pl.ds(1, 1)], pair, value_terms[2 * ROWS :])
    for copy in copies:
        copy.wait()


def held(array):
    return pltpu.VMEM(array.shape, array.dtype)


def call(kernel, outs, args, units, smem=0, in_specs=None, out_specs=None, scratch=()):
    moved = sum(a.size * a.dtype.itemsize for a in args)
    if in_specs is None:
        args = args[:smem] + [pltpu.with_memory_space_constraint(a, pltpu.VMEM) for a in args[smem:]]
    return pl.pallas_call(
        kernel,
        out_shape=outs,
        in_specs=in_specs or [SMEM] * smem + [VMEM] * (len(args) - smem),
        out_specs=out_specs or [VMEM] * len(outs),
        scratch_shapes=scratch,
        cost_estimate=pl.CostEstimate(
            flops=units * 2 * ROWS * ROWS * 1024, bytes_accessed=moved, transcendentals=0
        ),
        compiler_params=pltpu.CompilerParams(vmem_limit_bytes=32 * 2**20),
    )(*args)


def on_device(
    query_level, key_level, value_level, block_lists, query_column, key_column, grad_output
):
    size = lax.axis_size("lon")
    near = [(i, i ^ 1) for i in range(size)]
    far = [(i, (i + 1) % size if i % 2 else (i - 1) % size) for i in range(size)]
    level = jax.ShapeDtypeStruct(query_level.shape, BF16)
    level32 = jax.ShapeDtypeStruct(query_level.shape, F32)
    column = jax.ShapeDtypeStruct(query_column.shape, BF16)
    two = jax.ShapeDtypeStruct((2,) + query_level.shape[1:], BF16)
    weights = jax.ShapeDtypeStruct((PAIRS, 3 * ROWS, 2 * ROWS), BF16)
    given = [query_column, key_column, grad_output, key_level, value_level, query_level]
    grad_col, both, queries, col_queries, col_keys, col_grads = call(
        column_forward,
        [held(column), held(two), held(level), held(column), held(column), held(column)],
        [pltpu.with_memory_space_constraint(a, pltpu.HBM) for a in given],
        4,
        in_specs=[ANY] * 6,
        scratch=[pltpu.SemaphoreType.DMA((6,))],
    )
    both_far = lax.ppermute(both, "lon", far)
    both_near = lax.ppermute(both, "lon", near)
    grad_att = lax.all_to_all(grad_col, "lev", split_axis=0, concat_axis=1, tiled=True)
    grad_query, attended, dk, dv, near_terms, far_terms = call(
        level_kernel,
        [level, held(level), held(level32), held(level32), held(two), held(two)],
        [block_lists, queries, both, both_near, both_far, grad_att],
        18,
        smem=1,
        out_specs=[ANY] + [VMEM] * 5,
        scratch=[pltpu.VMEM(level.shape, BF16), pltpu.SemaphoreType.DMA((1, PAIRS))],
    )
    far_sums = lax.ppermute(far_terms, "lon", far)
    near_sums = lax.ppermute(near_terms, "lon", near)
    columns = lax.all_to_all(attended, "lev", split_axis=1, concat_axis=0, tiled=True)
    grad_query_column, grad_key_column, grad_key, grad_value = call(
        final_kernel,
        [column, column, level, level],
        [col_queries, col_keys, col_grads, columns, dk, dv, near_sums, far_sums],
        8,
        out_specs=[ANY] * 4,
        scratch=[pltpu.VMEM(column.shape, BF16)] * 2 + [pltpu.VMEM(level.shape, BF16)] * 2
        + [pltpu.SemaphoreType.DMA((4, PAIRS))],
    )
    return grad_query, grad_key, grad_value, grad_query_column, grad_key_column


def solution(mesh):
    level = P("lev", None, "lon", None)
    column = P(None, "lev", "lon", None)
    return jax.shard_map(
        on_device,
        mesh=mesh,
        in_specs=(level, level, level, P("lon", None, None), column, column, column),
        out_specs=(level, level, level, column, column),
        check_vma=False,
    )
```

time: 58.5 us -> 52.3 us (0.89)
  starting transfers between devices: 17.2 us -> 9.14 us
  blocking collectives: 23.7 us -> 27.4 us
  local copies, waits for them, and re-layouts: 2.88 us -> 0.67 us
    ppermute x8 -> x4, starting transfers between devices: 17.2 us -> 9.14 us  [the longest x1 4.79 us: on_device(): both_near = lax.ppermute(both, 'lon', near)]
    all_to_all x1, blocking collectives: 10.2 us -> 13.1 us  [on_device(): lax.all_to_all(attended, 'lev', split_axis=1, concat_axis=0, tiled=True)]
    unnamed x20 -> x2, local copies, waits for them, and re-layouts: 2.88 us -> 0.67 us
    all_to_all x1, blocking collectives: 13.6 us -> 14.4 us  [on_device(): lax.all_to_all(grad_col, 'lev', split_axis=0, concat_axis=1, tiled=True)]
    pallas_call x4 -> x3, Pallas kernels: 13.7 us -> 14.2 us  [call(): pl.pallas_call(kernel, out_shape=outs, in_specs=in_specs or [SMEM] * smem...]
  transfers between devices with their start and end apart: 8 -> 4, of which waited for: 0 -> 0; matrix products, arithmetic and copies ran while one was open for 0% -> 0% of each run, Pallas kernels for 7% -> 0%
where the time goes in v2:
time: 52.3 us; the launch traced here: 52.1 us
  blocking collectives  27.4 us (52%)
  Pallas kernels  14.2 us (27%)
  starting transfers between devices  9.14 us (17%)
  local copies, waits for them, and re-layouts  0.67 us (1%)
  between operations  0.66 us (1%)
    all_to_all x1, blocking collectives, on_device(): lax.all_to_all(grad_col, 'lev', split_axis=0, concat_axis=1, tiled=True)  14.4 us
    pallas_call x3, Pallas kernels, call(): pl.pallas_call(kernel, out_shape=outs, in_specs=in_specs or [SMEM] * smem...  14.2 us
    all_to_all x1, blocking collectives, on_device(): lax.all_to_all(attended, 'lev', split_axis=1, concat_axis=0, tiled=True)  13.1 us
    ppermute x1, starting transfers between devices, on_device(): both_near = lax.ppermute(both, 'lon', near)  4.79 us
    ppermute x1, starting transfers between devices, on_device(): both_far = lax.ppermute(both, 'lon', far)  3.11 us
    ppermute x1, starting transfers between devices, on_device(): near_sums = lax.ppermute(near_terms, 'lon', near)  1.24 us
  transfers between devices with their start and end apart: 4, of which 0 were waited for; matrix products, arithmetic and copies ran while one was open for 0% of the time, Pallas kernels for 0%

profile of v2, /device:TPU:1, one launch (start us, length us, event | category | flops | bytes accessed | tf_op | source)
XLA Modules:
  0.0 52.1 jit_solution(2052042640175968174)
XLA Ops:
  0.6 2.2 %shard_map.110 = (bf16[8,4,4,1024]{3,2,1,0:T(4,128)(2,1)S(1)}, bf16[2,32,4,1024]{3,2,1,0:T(4,128)(2,1)S(1)}, bf16[1,32,4,1024]{3,2,1,0:T(4,128)(2,1)S(1)}, bf16[...) custom-call(bf16[8,4,4,1024]{3,2,1,0:T(4,128)(2,1)} %q_hbm.1, ...), custom_call_target="tpu_custom_call" | custom-call | flops 134217728 | bytes 1572864 | tf_op jit(solution)/shard_map/pallas_call | solution.py:190
  2.9 3.1 %collective-permute-start.1 = (bf16[2,32,4,1024]{3,2,1,0:T(4,128)(2,1)S(1)}, bf16[2,32,4,1024]{3,2,1,0:T(4,128)(2,1)S(1)}, u32[]{:S(2)}, u32[]{:S(2)}) collective-permute-start(bf16[2,32,4,1024]{3,2,1,0:T(4,128)(2,1)S(1)} %get-tuple-element.22.both_ref), channel_id=1, source_target_pairs={{0,248},{8,16},{16,8},{24,32},{32,24},{40,48},{48,40},{56,64},{64,... | collective-permute-start | bytes 1572872 | tf_op jit(solution)/shard_map/ppermute | solution.py:223
  6.0 4.8 %collective-permute-start = (bf16[2,32,4,1024]{3,2,1,0:T(4,128)(2,1)S(1)}, bf16[2,32,4,1024]{3,2,1,0:T(4,128)(2,1)S(1)}, u32[]{:S(2)}, u32[]{:S(2)}) collective-permute-start(bf16[2,32,4,1024]{3,2,1,0:T(4,128)(2,1)S(1)} %get-tuple-element.22.both_ref), channel_id=1, source_target_pairs={{0,8},{8,0},{16,24},{24,16},{32,40},{40,32},{48,56},{56,48},{64,72... | collective-permute-start | bytes 1572872 | tf_op jit(solution)/shard_map/ppermute | solution.py:224
  10.8 14.4 %all_to_all.24 = bf16[8,4,4,1024]{3,2,1,0:T(4,128)(2,1)S(1)} all-to-all(bf16[8,4,4,1024]{3,2,1,0:T(4,128)(2,1)S(1)} %get-tuple-element.23), channel_id=1, replica_groups=mesh['lon'=32,'lev'=8] {'lev'}, dimensions={0} | all-to-all | bytes 524288 | tf_op jit(solution)/shard_map/all_to_all | solution.py:225
  25.1 0.0 copy-start
  25.1 0.0 collective-permute-done.1.far_ref
  25.1 0.0 collective-permute-done.near_ref
  25.1 0.7 %copy-done = s32[1,4,15]{2,1,0:T(4,128)S(1)} copy-done((s32[1,4,15]{2,1,0:T(4,128)S(1)}, s32[1,4,15]{2,1,0:T(4,128)}, u32[]{:S(2)}) %copy-start) | copy-done | bytes 264
  25.8 8.5 %shard_map.111 = (bf16[1,32,4,1024]{3,2,1,0:T(4,128)(2,1)}, bf16[1,32,4,1024]{3,2,1,0:T(4,128)(2,1)S(1)}, f32[1,32,4,1024]{3,2,1,0:T(4,128)S(1)}, f32[1,32,4,102...) custom-call(s32[1,4,15]{2,1,0:T(4,128)S(1)} %copy-done, ...), custom_call_target="tpu_custom_call" | custom-call | flops 603979776 | bytes 2097392 | tf_op jit(solution)/shard_map/pallas_call | solution.py:190
  34.3 1.2 %collective-permute-start.2 = (bf16[2,32,4,1024]{3,2,1,0:T(4,128)(2,1)S(1)}, bf16[2,32,4,1024]{3,2,1,0:T(4,128)(2,1)S(1)}, u32[]{:S(2)}, u32[]{:S(2)}) collective-permute-start(bf16[2,32,4,1024]{3,2,1,0:T(4,128)(2,1)S(1)} %get-tuple-element.31), channel_id=1, source_target_pairs={{0,8},{8,0},{16,24},{24,16},{32,40},{40,32},{48,56},{56,48},{64,72... | collective-permute-start | bytes 1572872 | tf_op jit(solution)/shard_map/ppermute | solution.py:236
  35.6 0.0 collective-permute-start.3
  35.6 13.1 %all_to_all.25 = bf16[1,32,4,1024]{3,2,0,1:T(4,128)(2,1)S(1)} all-to-all(bf16[1,32,4,1024]{3,2,0,1:T(4,128)(2,1)S(1)} %bitcast.4), channel_id=1, replica_groups=mesh['lon'=32,'lev'=8] {'lev'}, dimensions={1} | all-to-all | bytes 524288 | tf_op jit(solution)/shard_map/all_to_all | solution.py:237
  48.6 0.0 collective-permute-done.2.near_ref
  48.6 0.0 collective-permute-done.3.far_ref
  48.6 3.5 %shard_map.112 = (bf16[8,4,4,1024]{3,2,1,0:T(4,128)(2,1)}, bf16[8,4,4,1024]{3,2,1,0:T(4,128)(2,1)}, bf16[1,32,4,1024]{3,2,1,0:T(4,128)(2,1)}, bf16[1,32,4,1024]{3,2,1,0:T(4,128)(2,1)}) custom-call(bf16[8,4,4,1024]{3,2,1,0:T(4,128)(2,1)S(1)} %get-tuple-element.25.q_ref, bf16[8,4,4,1024]{3,2,1,0:T(4,128)(2,1)S(1)} %get-tuple-element.26.k_ref, ...), custom_call_target="tpu_custom_call" | custom-call | flops 268435456 | bytes 3145728 | tf_op jit(solution)/shard_map/pallas_call | solution.py:190
Async XLA Ops:
  2.9 22.3 %collective-permute-start.1 = (bf16[2,32,4,1024]{3,2,1,0:T(4,128)(2,1)S(1)}, bf16[2,32,4,1024]{3,2,1,0:T(4,128)(2,1)S(1)}, u32[]{:S(2)}, u32[]{:S(2)}) collective-permute-start(bf16[2,32,4,1024]{3,2,1,0:T(4,128)(2,1)S(1)} %get-tuple-element.22.both_ref), channel_id=1, source_target_pairs={{0,248},{8,16},{16,8},{24,32},{32,24},{40,48},{48,40},{56,64},{64,... | collective-permute-start | bytes 1572872 | tf_op jit(solution)/shard_map/ppermute | solution.py:223
  6.0 19.2 %collective-permute-start = (bf16[2,32,4,1024]{3,2,1,0:T(4,128)(2,1)S(1)}, bf16[2,32,4,1024]{3,2,1,0:T(4,128)(2,1)S(1)}, u32[]{:S(2)}, u32[]{:S(2)}) collective-permute-start(bf16[2,32,4,1024]{3,2,1,0:T(4,128)(2,1)S(1)} %get-tuple-element.22.both_ref), channel_id=1, source_target_pairs={{0,8},{8,0},{16,24},{24,16},{32,40},{40,32},{48,56},{56,48},{64,72... | collective-permute-start | bytes 1572872 | tf_op jit(solution)/shard_map/ppermute | solution.py:224
  25.1 0.7 %copy-start = (s32[1,4,15]{2,1,0:T(4,128)S(1)}, s32[1,4,15]{2,1,0:T(4,128)}, u32[]{:S(2)}) copy-start(s32[1,4,15]{2,1,0:T(4,128)} %lists_ref.1) | copy-start | bytes 724
  34.3 14.3 %collective-permute-start.2 = (bf16[2,32,4,1024]{3,2,1,0:T(4,128)(2,1)S(1)}, bf16[2,32,4,1024]{3,2,1,0:T(4,128)(2,1)S(1)}, u32[]{:S(2)}, u32[]{:S(2)}) collective-permute-start(bf16[2,32,4,1024]{3,2,1,0:T(4,128)(2,1)S(1)} %get-tuple-element.31), channel_id=1, source_target_pairs={{0,8},{8,0},{16,24},{24,16},{32,40},{40,32},{48,56},{56,48},{64,72... | collective-permute-start | bytes 1572872 | tf_op jit(solution)/shard_map/ppermute | solution.py:236
  35.6 13.1 %collective-permute-start.3 = (bf16[2,32,4,1024]{3,2,1,0:T(4,128)(2,1)S(1)}, bf16[2,32,4,1024]{3,2,1,0:T(4,128)(2,1)S(1)}, u32[]{:S(2)}, u32[]{:S(2)}) collective-permute-start(bf16[2,32,4,1024]{3,2,1,0:T(4,128)(2,1)S(1)} %get-tuple-element.32), channel_id=1, source_target_pairs={{0,248},{8,16},{16,8},{24,32},{32,24},{40,48},{48,40},{56,64},{64,... | collective-permute-start | bytes 1572872 | tf_op jit(solution)/shard_map/ppermute | solution.py:235

commit v3 on v2

v3 whole, which is shorter than its diff:
```python
import jax
import jax.numpy as jnp
from jax import lax
from jax.experimental import pallas as pl
from jax.experimental.pallas import tpu as pltpu
from jax.sharding import PartitionSpec as P

PAIRS = 8
ROWS = 128
PAIR = 128
NEGATIVE = -1e30
F32 = jnp.float32
BF16 = jnp.bfloat16

VMEM = pl.BlockSpec(memory_space=pltpu.VMEM)
ANY = pl.BlockSpec(memory_space=pl.ANY)


def tokens(ref, pair):
    return ref[:, :, :, pl.ds(pair * PAIR, PAIR)].reshape(ROWS, PAIR)


def put(ref, pair, value):
    shape = ref.shape[:-1] + (PAIR,)
    ref[:, :, :, pl.ds(pair * PAIR, PAIR)] = value.astype(ref.dtype).reshape(shape)


def both_heads(block):
    lane = lax.broadcasted_iota(jnp.int32, (1, PAIR), 1)
    first = (lane < PAIR // 2).astype(F32).astype(BF16)
    second = (lane >= PAIR // 2).astype(F32).astype(BF16)
    return jnp.concatenate([block * first, block * second], axis=0)


def outer(a, b):
    return lax.dot_general(a, b, (((1,), (1,)), ((), ())), preferred_element_type=F32)


def inner(a, b):
    return lax.dot_general(a, b, (((1,), (0,)), ((), ())), preferred_element_type=F32)


def own_features(both):
    half = PAIR // 2
    return jnp.concatenate([both[:half, :ROWS], both[half:, ROWS:]], axis=0)


def softmax_over_rows(scores):
    top = jnp.max(scores, axis=0, keepdims=True)
    raised = jnp.exp(scores - top)
    return raised * (1.0 / jnp.sum(raised, axis=0, keepdims=True))


def score_grads(probs, d_probs):
    return probs * (d_probs - jnp.sum(probs * d_probs, axis=0, keepdims=True))


def column_bias():
    key = lax.broadcasted_iota(jnp.int32, (ROWS, 2 * ROWS), 0)
    query = lax.broadcasted_iota(jnp.int32, (ROWS, 2 * ROWS), 1)
    return jnp.where((key & 15) == (query & 15), 0.0, NEGATIVE).astype(F32)


def pipelined(*stages):
    for step in range(PAIRS + len(stages) - 1):
        for delay in (0, 2, 1):
            if 0 <= step - delay < PAIRS:
                stages[delay](step - delay)


def level_bias(lists_ref):
    odd = lax.axis_index("lon") % 2
    lane = lax.broadcasted_iota(jnp.int32, (1, ROWS), 1)
    listed = jnp.zeros((1, ROWS), jnp.int32)
    for block in range(4):
        bits = jnp.int32(0)
        for j in range(15):
            bits = bits | lax.shift_left(jnp.int32(1), lists_ref[0, block, j])
        listed = jnp.where(lane // 32 == block, bits, listed)
    row = lax.broadcasted_iota(jnp.int32, (ROWS, ROWS), 0)
    block = (row // 32) * 6 + (row % 4) // 2
    parts = []
    for part in (2 - 2 * odd, 1, 2 * odd):
        allowed = lax.shift_right_logical(jnp.broadcast_to(listed, row.shape), block + 2 * part)
        parts.append(jnp.where((allowed & 1) == 1, 0.0, NEGATIVE).astype(F32))
    return jnp.concatenate(parts, axis=0)


def column_forward(
    lists_hbm, q_hbm, k_hbm, g_hbm, lk_hbm, lv_hbm, lq_hbm,
    out_ref, both_ref, lq_ref, q_ref, k_ref, g_ref, probs_ref, bias_ref,
    lists_ref, scores_ref, sems,
):
    moves = [
        (q_hbm, q_ref),
        (k_hbm, k_ref),
        (g_hbm, g_ref),
        (lists_hbm, lists_ref),
        (lk_hbm, both_ref.at[pl.ds(0, 1)]),
        (lv_hbm, both_ref.at[pl.ds(1, 1)]),
        (lq_hbm, lq_ref),
    ]
    copies = [
        pltpu.make_async_copy(src, dst, sems.at[i]) for i, (src, dst) in enumerate(moves)
    ]
    for copy in copies:
        copy.start()
    bias = column_bias()
    for copy in copies[:4]:
        copy.wait()

    def scores(pair):
        queries = both_heads(tokens(q_ref, pair) * BF16(0.125))
        scores_ref[pair % 2] = outer(tokens(k_ref, pair), queries)

    def softmax(pair):
        probs_ref[pair] = softmax_over_rows(scores_ref[pair % 2] + bias)

    def grads(pair):
        probs = probs_ref[pair].astype(BF16)
        put(out_ref, pair, inner(probs, both_heads(tokens(g_ref, pair))))

    pipelined(scores, softmax, grads)
    bias_ref[...] = level_bias(lists_ref)
    for copy in copies[4:]:
        copy.wait()


def send(pair, moves, sems):
    lanes = pl.ds(pair * PAIR, PAIR)
    copies = [
        pltpu.make_async_copy(src.at[:, :, :, lanes], dst.at[:, :, :, lanes], sems.at[i, pair])
        for i, (src, dst) in enumerate(moves)
    ]
    for copy in copies:
        copy.start()
    return copies


def final_kernel(
    q_ref, k_ref, g_ref, probs_ref, a_ref, dk_ref, dv_ref, near_ref, far_ref,
    dq_hbm, dkc_hbm, gk_hbm, gv_hbm, dqc_ref, dkc_ref, gk_ref, gv_ref, dp_ref, ds_ref, sems,
):
    copies = []

    def products(pair):
        dp_ref[pair % 2] = outer(tokens(a_ref, pair), both_heads(tokens(g_ref, pair)))

    def scores(pair):
        ds_ref[pair % 2] = score_grads(probs_ref[pair], dp_ref[pair % 2]).astype(BF16)

    def grads(pair):
        lanes = pl.ds(pair * PAIR, PAIR)
        d_scores = ds_ref[pair % 2]
        queries = both_heads(tokens(q_ref, pair) * BF16(0.125))
        put(dkc_ref, pair, inner(d_scores, queries))
        grad_query = own_features(inner(tokens(k_ref, pair).T, d_scores)) * 0.125
        put(dqc_ref, pair, grad_query.astype(BF16).T)
        for at, (own, out) in enumerate(((dk_ref, gk_ref), (dv_ref, gv_ref))):
            near = near_ref[pl.ds(at, 1), :, :, lanes].astype(F32)
            far = far_ref[pl.ds(at, 1), :, :, lanes].astype(F32)
            out[:, :, :, lanes] = (own[:, :, :, lanes] + (near + far)).astype(BF16)
        moves = [(dqc_ref, dq_hbm), (dkc_ref, dkc_hbm), (gk_ref, gk_hbm), (gv_ref, gv_hbm)]
        copies.extend(send(pair, moves, sems))

    pipelined(products, scores, grads)
    for copy in copies:
        copy.wait()


def halo(near, own, far, at, pair):
    return jnp.concatenate([tokens(r.at[pl.ds(at, 1)], pair) for r in (near, own, far)], axis=0)


def level_kernel(
    q_ref, both_ref, near_ref, far_ref, g_ref, bias_ref,
    dq_hbm, att_ref, dk_ref, dv_ref, near_out, far_out,
    dq_ref, s_ref, dp_ref, p_ref, ds_ref, qg_ref, kv_ref, sems,
):
    bias = jnp.concatenate([bias_ref[...], bias_ref[...]], axis=1)

    def products(pair):
        queries = both_heads(tokens(q_ref, pair) * BF16(0.125))
        grads = both_heads(tokens(g_ref, pair))
        keys = halo(near_ref, both_ref, far_ref, 0, pair)
        values = halo(near_ref, both_ref, far_ref, 1, pair)
        s_ref[pair % 2] = outer(keys, queries) + bias
        dp_ref[pair % 2] = outer(values, grads)
        qg_ref[pair % 4, 0] = queries
        qg_ref[pair % 4, 1] = grads
        kv_ref[pair % 4, 0] = keys.T
        kv_ref[pair % 4, 1] = values.T

    def scores(pair):
        probs = softmax_over_rows(s_ref[pair % 2])
        p_ref[pair % 2] = probs.astype(BF16)
        ds_ref[pair % 2] = score_grads(probs, dp_ref[pair % 2]).astype(BF16)

    def grads(pair):
        probs_b = p_ref[pair % 2]
        d_scores = ds_ref[pair % 2]
        attended = own_features(inner(kv_ref[pair % 4, 1], probs_b))
        grad_query = own_features(inner(kv_ref[pair % 4, 0], d_scores)) * 0.125
        key_terms = inner(d_scores, qg_ref[pair % 4, 0])
        value_terms = inner(probs_b, qg_ref[pair % 4, 1])
        put(att_ref, pair, attended.astype(BF16).T)
        put(dq_ref, pair, grad_query.astype(BF16).T)
        put(near_out.at[pl.ds(0, 1)], pair, key_terms[:ROWS])
        put(near_out.at[pl.ds(1, 1)], pair, value_terms[:ROWS])
        put(dk_ref, pair, key_terms[ROWS : 2 * ROWS])
        put(dv_ref, pair, value_terms[ROWS : 2 * ROWS])
        put(far_out.at[pl.ds(0, 1)], pair, key_terms[2 * ROWS :])
        put(far_out.at[pl.ds(1, 1)], pair, value_terms[2 * ROWS :])

    pipelined(products, scores, grads)
    copy = pltpu.make_async_copy(dq_ref, dq_hbm, sems.at[0])
    copy.start()
    copy.wait()


def held(array):
    return pltpu.VMEM(array.shape, array.dtype)


def call(kernel, outs, args, units, in_specs=None, out_specs=None, scratch=()):
    moved = sum(a.size * a.dtype.itemsize for a in args)
    if in_specs is None:
        args = [pltpu.with_memory_space_constraint(a, pltpu.VMEM) for a in args]
    return pl.pallas_call(
        kernel,
        out_shape=outs,
        in_specs=in_specs or [VMEM] * len(args),
        out_specs=out_specs or [VMEM] * len(outs),
        scratch_shapes=scratch,
        cost_estimate=pl.CostEstimate(
            flops=units * 2 * ROWS * ROWS * 1024, bytes_accessed=moved, transcendentals=0
        ),
        compiler_params=pltpu.CompilerParams(vmem_limit_bytes=32 * 2**20),
    )(*args)


def on_device(
    query_level, key_level, value_level, block_lists, query_column, key_column, grad_output
):
    size = lax.axis_size("lon")
    near = [(i, i ^ 1) for i in range(size)]
    far = [(i, (i + 1) % size if i % 2 else (i - 1) % size) for i in range(size)]
    level = jax.ShapeDtypeStruct(query_level.shape, BF16)
    level32 = jax.ShapeDtypeStruct(query_level.shape, F32)
    column = jax.ShapeDtypeStruct(query_column.shape, BF16)
    two = jax.ShapeDtypeStruct((2,) + query_level.shape[1:], BF16)
    col_probs = jax.ShapeDtypeStruct((PAIRS, ROWS, 2 * ROWS), F32)
    mask = jax.ShapeDtypeStruct((3 * ROWS, ROWS), F32)
    given = [
        block_lists, query_column, key_column, grad_output, key_level, value_level, query_level,
    ]
    grad_col, both, queries, col_queries, col_keys, col_grads, probs, bias = call(
        column_forward,
        [held(a) for a in (column, two, level, column, column, column, col_probs, mask)],
        [pltpu.with_memory_space_constraint(a, pltpu.HBM) for a in given],
        4,
        in_specs=[ANY] * 7,
        scratch=[
            pltpu.SMEM(block_lists.shape, jnp.int32),
            pltpu.VMEM((2, ROWS, 2 * ROWS), F32),
            pltpu.SemaphoreType.DMA((7,)),
        ],
    )
    both_far = lax.ppermute(both, "lon", far)
    both_near = lax.ppermute(both, "lon", near)
    grad_att = lax.all_to_all(grad_col, "lev", split_axis=0, concat_axis=1, tiled=True)
    grad_query, attended, dk, dv, near_terms, far_terms = call(
        level_kernel,
        [level] + [held(a) for a in (level, level32, level32, two, two)],
        [queries, both, both_near, both_far, grad_att, bias],
        18,
        out_specs=[ANY] + [VMEM] * 5,
        scratch=[
            pltpu.VMEM(level.shape, BF16),
            pltpu.VMEM((2, 3 * ROWS, 2 * ROWS), F32),
            pltpu.VMEM((2, 3 * ROWS, 2 * ROWS), F32),
            pltpu.VMEM((2, 3 * ROWS, 2 * ROWS), BF16),
            pltpu.VMEM((2, 3 * ROWS, 2 * ROWS), BF16),
            pltpu.VMEM((4, 2, 2 * ROWS, PAIR), BF16),
            pltpu.VMEM((4, 2, PAIR, 3 * ROWS), BF16),
            pltpu.SemaphoreType.DMA((1,)),
        ],
    )
    far_sums = lax.ppermute(far_terms, "lon", far)
    near_sums = lax.ppermute(near_terms, "lon", near)
    columns = lax.all_to_all(attended, "lev", split_axis=1, concat_axis=0, tiled=True)
    grad_query_column, grad_key_column, grad_key, grad_value = call(
        final_kernel,
        [column, column, level, level],
        [col_queries, col_keys, col_grads, probs, columns, dk, dv, near_sums, far_sums],
        8,
        out_specs=[ANY] * 4,
        scratch=[pltpu.VMEM(column.shape, BF16)] * 2
        + [pltpu.VMEM(level.shape, BF16)] * 2
        + [pltpu.VMEM((2, ROWS, 2 * ROWS), F32), pltpu.VMEM((2, ROWS, 2 * ROWS), BF16)]
        + [pltpu.SemaphoreType.DMA((4, PAIRS))],
    )
    return grad_query, grad_key, grad_value, grad_query_column, grad_key_column


def solution(mesh):
    level = P("lev", None, "lon", None)
    column = P(None, "lev", "lon", None)
    return jax.shard_map(
        on_device,
        mesh=mesh,
        in_specs=(level, level, level, P("lon", None, None), column, column, column),
        out_specs=(level, level, level, column, column),
        check_vma=False,
    )
```

time: 52.3 us -> 46.1 us (0.88)
  Pallas kernels: 14.2 us -> 8.72 us
  local copies, waits for them, and re-layouts: 0.67 us -> 0 us
    pallas_call x3, Pallas kernels: 14.2 us -> 8.72 us  [call(): pl.pallas_call(kernel, out_shape=outs, in_specs=in_specs or [VMEM] * len(...]
    unnamed x2 -> x0, local copies, waits for them, and re-layouts: 0.67 us -> none
where the time goes in v3:
time: 46.1 us; the launch traced here: 46 us
  blocking collectives  27.4 us (59%)
  starting transfers between devices  9.14 us (20%)
  Pallas kernels  8.72 us (19%)
  between operations  0.66 us (1%)
    all_to_all x1, blocking collectives, on_device(): lax.all_to_all(grad_col, 'lev', split_axis=0, concat_axis=1, tiled=True)  14.4 us
    all_to_all x1, blocking collectives, on_device(): lax.all_to_all(attended, 'lev', split_axis=1, concat_axis=0, tiled=True)  13.1 us
    pallas_call x3, Pallas kernels, call(): pl.pallas_call(kernel, out_shape=outs, in_specs=in_specs or [VMEM] * len(...  8.72 us
    ppermute x1, starting transfers between devices, on_device(): both_near = lax.ppermute(both, 'lon', near)  4.79 us
    ppermute x1, starting transfers between devices, on_device(): both_far = lax.ppermute(both, 'lon', far)  3.11 us
    ppermute x1, starting transfers between devices, on_device(): near_sums = lax.ppermute(near_terms, 'lon', near)  1.24 us
  transfers between devices with their start and end apart: 4, of which 0 were waited for; matrix products, arithmetic and copies ran while one was open for 0% of the time, Pallas kernels for 0%

profile of v3, /device:TPU:1, one launch (start us, length us, event | category | flops | bytes accessed | tf_op | source)
XLA Modules:
  0.0 46.0 jit_solution(6994967631898475686)
XLA Ops:
  0.6 2.1 %shard_map.110 = (bf16[8,4,4,1024]{3,2,1,0:T(4,128)(2,1)S(1)}, bf16[2,32,4,1024]{3,2,1,0:T(4,128)(2,1)S(1)}, bf16[1,32,4,1024]{3,2,1,0:T(4,128)(2,1)S(1)}, bf16[...) custom-call(s32[1,4,15]{2,1,0:T(4,128)} %lists_hbm.1, ...), custom_call_target="tpu_custom_call" | custom-call | flops 134217728 | bytes 1573104 | tf_op jit(solution)/shard_map/pallas_call | solution.py:229
  2.7 3.1 %collective-permute-start.1 = (bf16[2,32,4,1024]{3,2,1,0:T(4,128)(2,1)S(1)}, bf16[2,32,4,1024]{3,2,1,0:T(4,128)(2,1)S(1)}, u32[]{:S(2)}, u32[]{:S(2)}) collective-permute-start(bf16[2,32,4,1024]{3,2,1,0:T(4,128)(2,1)S(1)} %get-tuple-element.24.both_ref), channel_id=1, source_target_pairs={{0,248},{8,16},{16,8},{24,32},{32,24},{40,48},{48,40},{56,64},{64,... | collective-permute-start | bytes 1572872 | tf_op jit(solution)/shard_map/ppermute | solution.py:269
  5.9 4.8 %collective-permute-start = (bf16[2,32,4,1024]{3,2,1,0:T(4,128)(2,1)S(1)}, bf16[2,32,4,1024]{3,2,1,0:T(4,128)(2,1)S(1)}, u32[]{:S(2)}, u32[]{:S(2)}) collective-permute-start(bf16[2,32,4,1024]{3,2,1,0:T(4,128)(2,1)S(1)} %get-tuple-element.24.both_ref), channel_id=1, source_target_pairs={{0,8},{8,0},{16,24},{24,16},{32,40},{40,32},{48,56},{56,48},{64,72... | collective-permute-start | bytes 1572872 | tf_op jit(solution)/shard_map/ppermute | solution.py:270
  10.6 14.4 %all_to_all.24 = bf16[8,4,4,1024]{3,2,1,0:T(4,128)(2,1)S(1)} all-to-all(bf16[8,4,4,1024]{3,2,1,0:T(4,128)(2,1)S(1)} %get-tuple-element.25), channel_id=1, replica_groups=mesh['lon'=32,'lev'=8] {'lev'}, dimensions={0} | all-to-all | bytes 524288 | tf_op jit(solution)/shard_map/all_to_all | solution.py:271
  25.0 0.0 collective-permute-done.1.far_ref
  25.0 0.0 collective-permute-done.near_ref
  25.0 4.2 %shard_map.111 = (bf16[1,32,4,1024]{3,2,1,0:T(4,128)(2,1)}, bf16[1,32,4,1024]{3,2,1,0:T(4,128)(2,1)S(1)}, f32[1,32,4,1024]{3,2,1,0:T(4,128)S(1)}, f32[1,32,4,102...) custom-call(bf16[1,32,4,1024]{3,2,1,0:T(4,128)(2,1)S(1)} %get-tuple-element.23.q_ref, ...), custom_call_target="tpu_custom_call" | custom-call | flops 603979776 | bytes 2293760 | tf_op jit(solution)/shard_map/pallas_call | solution.py:229
  29.2 1.2 %collective-permute-start.2 = (bf16[2,32,4,1024]{3,2,1,0:T(4,128)(2,1)S(1)}, bf16[2,32,4,1024]{3,2,1,0:T(4,128)(2,1)S(1)}, u32[]{:S(2)}, u32[]{:S(2)}) collective-permute-start(bf16[2,32,4,1024]{3,2,1,0:T(4,128)(2,1)S(1)} %get-tuple-element.35), channel_id=1, source_target_pairs={{0,8},{8,0},{16,24},{24,16},{32,40},{40,32},{48,56},{56,48},{64,72... | collective-permute-start | bytes 1572872 | tf_op jit(solution)/shard_map/ppermute | solution.py:290
  30.4 0.0 collective-permute-start.3
  30.4 13.1 %all_to_all.25 = bf16[1,32,4,1024]{3,2,0,1:T(4,128)(2,1)S(1)} all-to-all(bf16[1,32,4,1024]{3,2,0,1:T(4,128)(2,1)S(1)} %bitcast.5), channel_id=1, replica_groups=mesh['lon'=32,'lev'=8] {'lev'}, dimensions={1} | all-to-all | bytes 524288 | tf_op jit(solution)/shard_map/all_to_all | solution.py:291
  43.5 0.0 collective-permute-done.2.near_ref
  43.5 0.0 collective-permute-done.3.far_ref
  43.5 2.4 %shard_map.112 = (bf16[8,4,4,1024]{3,2,1,0:T(4,128)(2,1)}, bf16[8,4,4,1024]{3,2,1,0:T(4,128)(2,1)}, bf16[1,32,4,1024]{3,2,1,0:T(4,128)(2,1)}, bf16[1,32,4,1024]{3,2,1,0:T(4,128)(2,1)}) custom-call(bf16[8,4,4,1024]{3,2,1,0:T(4,128)(2,1)S(1)} %get-tuple-element.28.q_ref, bf16[8,4,4,1024]{3,2,1,0:T(4,128)(2,1)S(1)} %get-tuple-element.29.k_ref, ...), custom_call_target="tpu_custom_call" | custom-call | flops 268435456 | bytes 4194304 | tf_op jit(solution)/shard_map/pallas_call | solution.py:229
Async XLA Ops:
  2.7 22.3 %collective-permute-start.1 = (bf16[2,32,4,1024]{3,2,1,0:T(4,128)(2,1)S(1)}, bf16[2,32,4,1024]{3,2,1,0:T(4,128)(2,1)S(1)}, u32[]{:S(2)}, u32[]{:S(2)}) collective-permute-start(bf16[2,32,4,1024]{3,2,1,0:T(4,128)(2,1)S(1)} %get-tuple-element.24.both_ref), channel_id=1, source_target_pairs={{0,248},{8,16},{16,8},{24,32},{32,24},{40,48},{48,40},{56,64},{64,... | collective-permute-start | bytes 1572872 | tf_op jit(solution)/shard_map/ppermute | solution.py:269
  5.9 19.2 %collective-permute-start = (bf16[2,32,4,1024]{3,2,1,0:T(4,128)(2,1)S(1)}, bf16[2,32,4,1024]{3,2,1,0:T(4,128)(2,1)S(1)}, u32[]{:S(2)}, u32[]{:S(2)}) collective-permute-start(bf16[2,32,4,1024]{3,2,1,0:T(4,128)(2,1)S(1)} %get-tuple-element.24.both_ref), channel_id=1, source_target_pairs={{0,8},{8,0},{16,24},{24,16},{32,40},{40,32},{48,56},{56,48},{64,72... | collective-permute-start | bytes 1572872 | tf_op jit(solution)/shard_map/ppermute | solution.py:270
  29.2 14.3 %collective-permute-start.2 = (bf16[2,32,4,1024]{3,2,1,0:T(4,128)(2,1)S(1)}, bf16[2,32,4,1024]{3,2,1,0:T(4,128)(2,1)S(1)}, u32[]{:S(2)}, u32[]{:S(2)}) collective-permute-start(bf16[2,32,4,1024]{3,2,1,0:T(4,128)(2,1)S(1)} %get-tuple-element.35), channel_id=1, source_target_pairs={{0,8},{8,0},{16,24},{24,16},{32,40},{40,32},{48,56},{56,48},{64,72... | collective-permute-start | bytes 1572872 | tf_op jit(solution)/shard_map/ppermute | solution.py:290
  30.4 13.1 %collective-permute-start.3 = (bf16[2,32,4,1024]{3,2,1,0:T(4,128)(2,1)S(1)}, bf16[2,32,4,1024]{3,2,1,0:T(4,128)(2,1)S(1)}, u32[]{:S(2)}, u32[]{:S(2)}) collective-permute-start(bf16[2,32,4,1024]{3,2,1,0:T(4,128)(2,1)S(1)} %get-tuple-element.36), channel_id=1, source_target_pairs={{0,248},{8,16},{16,8},{24,32},{32,24},{40,48},{48,40},{56,64},{64,... | collective-permute-start | bytes 1572872 | tf_op jit(solution)/shard_map/ppermute | solution.py:289

commit v4 on v3

--- a/solution.py
+++ b/solution.py
@@ -92,10 +92,10 @@
     lists_ref, scores_ref, sems,
 ):
     moves = [
+        (lists_hbm, lists_ref),
         (q_hbm, q_ref),
         (k_hbm, k_ref),
         (g_hbm, g_ref),
-        (lists_hbm, lists_ref),
         (lk_hbm, both_ref.at[pl.ds(0, 1)]),
         (lv_hbm, both_ref.at[pl.ds(1, 1)]),
         (lq_hbm, lq_ref),
@@ -105,8 +105,10 @@
     ]
     for copy in copies:
         copy.start()
+    copies[0].wait()
+    bias_ref[...] = level_bias(lists_ref)
     bias = column_bias()
-    for copy in copies[:4]:
+    for copy in copies[1:4]:
         copy.wait()
 
     def scores(pair):
@@ -121,7 +123,6 @@
         put(out_ref, pair, inner(probs, both_heads(tokens(g_ref, pair))))
 
     pipelined(scores, softmax, grads)
-    bias_ref[...] = level_bias(lists_ref)
     for copy in copies[4:]:
         copy.wait()
 
@@ -138,10 +139,12 @@
 
 
 def final_kernel(
-    q_ref, k_ref, g_ref, probs_ref, a_ref, dk_ref, dv_ref, near_ref, far_ref,
-    dq_hbm, dkc_hbm, gk_hbm, gv_hbm, dqc_ref, dkc_ref, gk_ref, gv_ref, dp_ref, ds_ref, sems,
+    q_ref, k_ref, g_ref, probs_ref, a_ref, dk_ref, dv_ref, near_ref, far_ref, lq_ref,
+    dq_hbm, dkc_hbm, gk_hbm, gv_hbm, lq_hbm,
+    dqc_ref, dkc_ref, gk_ref, gv_ref, dp_ref, ds_ref, sems, lq_sem,
 ):
-    copies = []
+    copies = [pltpu.make_async_copy(lq_ref, lq_hbm, lq_sem.at[0])]
+    copies[0].start()
 
     def products(pair):
         dp_ref[pair % 2] = outer(tokens(a_ref, pair), both_heads(tokens(g_ref, pair)))
@@ -174,8 +177,8 @@
 
 def level_kernel(
     q_ref, both_ref, near_ref, far_ref, g_ref, bias_ref,
-    dq_hbm, att_ref, dk_ref, dv_ref, near_out, far_out,
-    dq_ref, s_ref, dp_ref, p_ref, ds_ref, qg_ref, kv_ref, sems,
+    dq_ref, att_ref, dk_ref, dv_ref, near_out, far_out,
+    s_ref, dp_ref, p_ref, ds_ref, qg_ref, kv_ref,
 ):
     bias = jnp.concatenate([bias_ref[...], bias_ref[...]], axis=1)
 
@@ -213,9 +216,6 @@
         put(far_out.at[pl.ds(1, 1)], pair, value_terms[2 * ROWS :])
 
     pipelined(products, scores, grads)
-    copy = pltpu.make_async_copy(dq_ref, dq_hbm, sems.at[0])
-    copy.start()
-    copy.wait()
 
 
 def held(array):
@@ -266,39 +266,39 @@
             pltpu.SemaphoreType.DMA((7,)),
         ],
     )
+    both_near = lax.ppermute(both, "lon", near)
     both_far = lax.ppermute(both, "lon", far)
-    both_near = lax.ppermute(both, "lon", near)
     grad_att = lax.all_to_all(grad_col, "lev", split_axis=0, concat_axis=1, tiled=True)
     grad_query, attended, dk, dv, near_terms, far_terms = call(
         level_kernel,
-        [level] + [held(a) for a in (level, level32, level32, two, two)],
+        [held(a) for a in (level, level, level32, level32, two, two)],
         [queries, both, both_near, both_far, grad_att, bias],
         18,
-        out_specs=[ANY] + [VMEM] * 5,
         scratch=[
-            pltpu.VMEM(level.shape, BF16),
             pltpu.VMEM((2, 3 * ROWS, 2 * ROWS), F32),
             pltpu.VMEM((2, 3 * ROWS, 2 * ROWS), F32),
             pltpu.VMEM((2, 3 * ROWS, 2 * ROWS), BF16),
             pltpu.VMEM((2, 3 * ROWS, 2 * ROWS), BF16),
             pltpu.VMEM((4, 2, 2 * ROWS, PAIR), BF16),
             pltpu.VMEM((4, 2, PAIR, 3 * ROWS), BF16),
-            pltpu.SemaphoreType.DMA((1,)),
         ],
     )
     far_sums = lax.ppermute(far_terms, "lon", far)
     near_sums = lax.ppermute(near_terms, "lon", near)
     columns = lax.all_to_all(attended, "lev", split_axis=1, concat_axis=0, tiled=True)
-    grad_query_column, grad_key_column, grad_key, grad_value = call(
+    grad_query_column, grad_key_column, grad_key, grad_value, grad_query = call(
         final_kernel,
-        [column, column, level, level],
-        [col_queries, col_keys, col_grads, probs, columns, dk, dv, near_sums, far_sums],
+        [column, column, level, level, level],
+        [
+            col_queries, col_keys, col_grads, probs, columns,
+            dk, dv, near_sums, far_sums, grad_query,
+        ],
         8,
-        out_specs=[ANY] * 4,
+        out_specs=[ANY] * 5,
         scratch=[pltpu.VMEM(column.shape, BF16)] * 2
         + [pltpu.VMEM(level.shape, BF16)] * 2
         + [pltpu.VMEM((2, ROWS, 2 * ROWS), F32), pltpu.VMEM((2, ROWS, 2 * ROWS), BF16)]
-        + [pltpu.SemaphoreType.DMA((4, PAIRS))],
+        + [pltpu.SemaphoreType.DMA((4, PAIRS)), pltpu.SemaphoreType.DMA((1,))],
     )
     return grad_query, grad_key, grad_value, grad_query_column, grad_key_column
 

time: 46.1 us -> 45.4 us (0.985)
  Pallas kernels: 8.72 us -> 8 us
    pallas_call x3, Pallas kernels: 8.72 us -> 8 us  [call(): pl.pallas_call(kernel, out_shape=outs, in_specs=in_specs or [VMEM] * len(...]
where the time goes in v4:
time: 45.4 us; the launch traced here: 45.2 us
  blocking collectives  27.4 us (60%)
  starting transfers between devices  9.14 us (20%)
  Pallas kernels  8 us (18%)
  between operations  0.65 us (1%)
    all_to_all x1, blocking collectives, on_device(): lax.all_to_all(grad_col, 'lev', split_axis=0, concat_axis=1, tiled=True)  14.4 us
    all_to_all x1, blocking collectives, on_device(): lax.all_to_all(attended, 'lev', split_axis=1, concat_axis=0, tiled=True)  13.1 us
    pallas_call x3, Pallas kernels, call(): pl.pallas_call(kernel, out_shape=outs, in_specs=in_specs or [VMEM] * len(...  8 us
    ppermute x1, starting transfers between devices, on_device(): both_near = lax.ppermute(both, 'lon', near)  4.79 us
    ppermute x1, starting transfers between devices, on_device(): both_far = lax.ppermute(both, 'lon', far)  3.11 us
    ppermute x1, starting transfers between devices, on_device(): near_sums = lax.ppermute(near_terms, 'lon', near)  1.24 us
  transfers between devices with their start and end apart: 4, of which 0 were waited for; matrix products, arithmetic and copies ran while one was open for 0% of the time, Pallas kernels for 0%

profile of v4, /device:TPU:1, one launch (start us, length us, event | category | flops | bytes accessed | tf_op | source)
XLA Modules:
  0.0 45.2 jit_solution(16335277052061801020)
XLA Ops:
  0.6 2.1 %shard_map.110 = (bf16[8,4,4,1024]{3,2,1,0:T(4,128)(2,1)S(1)}, bf16[2,32,4,1024]{3,2,1,0:T(4,128)(2,1)S(1)}, bf16[1,32,4,1024]{3,2,1,0:T(4,128)(2,1)S(1)}, bf16[...) custom-call(s32[1,4,15]{2,1,0:T(4,128)} %lists_hbm.1, ...), custom_call_target="tpu_custom_call" | custom-call | flops 134217728 | bytes 1573104 | tf_op jit(solution)/shard_map/pallas_call | solution.py:229
  2.7 3.1 %collective-permute-start.1 = (bf16[2,32,4,1024]{3,2,1,0:T(4,128)(2,1)S(1)}, bf16[2,32,4,1024]{3,2,1,0:T(4,128)(2,1)S(1)}, u32[]{:S(2)}, u32[]{:S(2)}) collective-permute-start(bf16[2,32,4,1024]{3,2,1,0:T(4,128)(2,1)S(1)} %get-tuple-element.29.both_ref), channel_id=1, source_target_pairs={{0,248},{8,16},{16,8},{24,32},{32,24},{40,48},{48,40},{56,64},{64,... | collective-permute-start | bytes 1572872 | tf_op jit(solution)/shard_map/ppermute | solution.py:270
  5.8 4.8 %collective-permute-start = (bf16[2,32,4,1024]{3,2,1,0:T(4,128)(2,1)S(1)}, bf16[2,32,4,1024]{3,2,1,0:T(4,128)(2,1)S(1)}, u32[]{:S(2)}, u32[]{:S(2)}) collective-permute-start(bf16[2,32,4,1024]{3,2,1,0:T(4,128)(2,1)S(1)} %get-tuple-element.29.both_ref), channel_id=1, source_target_pairs={{0,8},{8,0},{16,24},{24,16},{32,40},{40,32},{48,56},{56,48},{64,72... | collective-permute-start | bytes 1572872 | tf_op jit(solution)/shard_map/ppermute | solution.py:269
  10.6 14.4 %all_to_all.24 = bf16[8,4,4,1024]{3,2,1,0:T(4,128)(2,1)S(1)} all-to-all(bf16[8,4,4,1024]{3,2,1,0:T(4,128)(2,1)S(1)} %get-tuple-element.30), channel_id=1, replica_groups=mesh['lon'=32,'lev'=8] {'lev'}, dimensions={0} | all-to-all | bytes 524288 | tf_op jit(solution)/shard_map/all_to_all | solution.py:271
  25.0 0.0 collective-permute-done.1.far_ref
  25.0 0.0 collective-permute-done.near_ref
  25.0 3.5 %shard_map.111 = (bf16[1,32,4,1024]{3,2,1,0:T(4,128)(2,1)S(1)}, bf16[1,32,4,1024]{3,2,1,0:T(4,128)(2,1)S(1)}, f32[1,32,4,1024]{3,2,1,0:T(4,128)S(1)}, f32[1,32,4...) custom-call(bf16[1,32,4,1024]{3,2,1,0:T(4,128)(2,1)S(1)} %get-tuple-element.28.q_ref, ...), custom_call_target="tpu_custom_call" | custom-call | flops 603979776 | bytes 2293760 | tf_op jit(solution)/shard_map/pallas_call | solution.py:229
  28.5 1.2 %collective-permute-start.2 = (bf16[2,32,4,1024]{3,2,1,0:T(4,128)(2,1)S(1)}, bf16[2,32,4,1024]{3,2,1,0:T(4,128)(2,1)S(1)}, u32[]{:S(2)}, u32[]{:S(2)}) collective-permute-start(bf16[2,32,4,1024]{3,2,1,0:T(4,128)(2,1)S(1)} %get-tuple-element.35), channel_id=1, source_target_pairs={{0,8},{8,0},{16,24},{24,16},{32,40},{40,32},{48,56},{56,48},{64,72... | collective-permute-start | bytes 1572872 | tf_op jit(solution)/shard_map/ppermute | solution.py:287
  29.7 0.0 collective-permute-start.3
  29.7 13.1 %all_to_all.25 = bf16[1,32,4,1024]{3,2,0,1:T(4,128)(2,1)S(1)} all-to-all(bf16[1,32,4,1024]{3,2,0,1:T(4,128)(2,1)S(1)} %bitcast.5), channel_id=1, replica_groups=mesh['lon'=32,'lev'=8] {'lev'}, dimensions={1} | all-to-all | bytes 524288 | tf_op jit(solution)/shard_map/all_to_all | solution.py:288
  42.8 0.0 collective-permute-done.2.near_ref
  42.8 0.0 collective-permute-done.3.far_ref
  42.8 2.5 %shard_map.112 = (bf16[8,4,4,1024]{3,2,1,0:T(4,128)(2,1)}, bf16[8,4,4,1024]{3,2,1,0:T(4,128)(2,1)}, bf16[1,32,4,1024]{3,2,1,0:T(4,128)(2,1)}, bf16[1,32,4,1024]{3,2,1,0:T(4,128)(2,1)}, bf16[1,32,4,1024]{3,2,1,0:T(4,128)(2,1)}) custom-call(bf16[8,4,4,1024]{3,2,1,0:T(4,128)(2,1)S(1)} %get-tuple-element.24.q_ref, ...), custom_call_target="tpu_custom_call" | custom-call | flops 268435456 | bytes 4456448 | tf_op jit(solution)/shard_map/pallas_call | solution.py:229
Async XLA Ops:
  2.7 22.3 %collective-permute-start.1 = (bf16[2,32,4,1024]{3,2,1,0:T(4,128)(2,1)S(1)}, bf16[2,32,4,1024]{3,2,1,0:T(4,128)(2,1)S(1)}, u32[]{:S(2)}, u32[]{:S(2)}) collective-permute-start(bf16[2,32,4,1024]{3,2,1,0:T(4,128)(2,1)S(1)} %get-tuple-element.29.both_ref), channel_id=1, source_target_pairs={{0,248},{8,16},{16,8},{24,32},{32,24},{40,48},{48,40},{56,64},{64,... | collective-permute-start | bytes 1572872 | tf_op jit(solution)/shard_map/ppermute | solution.py:270
  5.8 19.2 %collective-permute-start = (bf16[2,32,4,1024]{3,2,1,0:T(4,128)(2,1)S(1)}, bf16[2,32,4,1024]{3,2,1,0:T(4,128)(2,1)S(1)}, u32[]{:S(2)}, u32[]{:S(2)}) collective-permute-start(bf16[2,32,4,1024]{3,2,1,0:T(4,128)(2,1)S(1)} %get-tuple-element.29.both_ref), channel_id=1, source_target_pairs={{0,8},{8,0},{16,24},{24,16},{32,40},{40,32},{48,56},{56,48},{64,72... | collective-permute-start | bytes 1572872 | tf_op jit(solution)/shard_map/ppermute | solution.py:269
  28.5 14.3 %collective-permute-start.2 = (bf16[2,32,4,1024]{3,2,1,0:T(4,128)(2,1)S(1)}, bf16[2,32,4,1024]{3,2,1,0:T(4,128)(2,1)S(1)}, u32[]{:S(2)}, u32[]{:S(2)}) collective-permute-start(bf16[2,32,4,1024]{3,2,1,0:T(4,128)(2,1)S(1)} %get-tuple-element.35), channel_id=1, source_target_pairs={{0,8},{8,0},{16,24},{24,16},{32,40},{40,32},{48,56},{56,48},{64,72... | collective-permute-start | bytes 1572872 | tf_op jit(solution)/shard_map/ppermute | solution.py:287
  29.7 13.1 %collective-permute-start.3 = (bf16[2,32,4,1024]{3,2,1,0:T(4,128)(2,1)S(1)}, bf16[2,32,4,1024]{3,2,1,0:T(4,128)(2,1)S(1)}, u32[]{:S(2)}, u32[]{:S(2)}) collective-permute-start(bf16[2,32,4,1024]{3,2,1,0:T(4,128)(2,1)S(1)} %get-tuple-element.36), channel_id=1, source_target_pairs={{0,248},{8,16},{16,8},{24,32},{32,24},{40,48},{48,40},{56,64},{64,... | collective-permute-start | bytes 1572872 | tf_op jit(solution)/shard_map/ppermute | solution.py:286

commit v5 on v4

--- a/solution.py
+++ b/solution.py
@@ -127,23 +127,12 @@
         copy.wait()
 
 
-def send(pair, moves, sems):
-    lanes = pl.ds(pair * PAIR, PAIR)
-    copies = [
-        pltpu.make_async_copy(src.at[:, :, :, lanes], dst.at[:, :, :, lanes], sems.at[i, pair])
-        for i, (src, dst) in enumerate(moves)
-    ]
-    for copy in copies:
-        copy.start()
-    return copies
-
-
 def final_kernel(
     q_ref, k_ref, g_ref, probs_ref, a_ref, dk_ref, dv_ref, near_ref, far_ref, lq_ref,
     dq_hbm, dkc_hbm, gk_hbm, gv_hbm, lq_hbm,
-    dqc_ref, dkc_ref, gk_ref, gv_ref, dp_ref, ds_ref, sems, lq_sem,
+    dqc_ref, dkc_ref, gk_ref, gv_ref, dp_ref, ds_ref, sems,
 ):
-    copies = [pltpu.make_async_copy(lq_ref, lq_hbm, lq_sem.at[0])]
+    copies = [pltpu.make_async_copy(lq_ref, lq_hbm, sems.at[0])]
     copies[0].start()
 
     def products(pair):
@@ -153,30 +142,32 @@
         ds_ref[pair % 2] = score_grads(probs_ref[pair], dp_ref[pair % 2]).astype(BF16)
 
     def grads(pair):
-        lanes = pl.ds(pair * PAIR, PAIR)
         d_scores = ds_ref[pair % 2]
         queries = both_heads(tokens(q_ref, pair) * BF16(0.125))
         put(dkc_ref, pair, inner(d_scores, queries))
         grad_query = own_features(inner(tokens(k_ref, pair).T, d_scores)) * 0.125
         put(dqc_ref, pair, grad_query.astype(BF16).T)
-        for at, (own, out) in enumerate(((dk_ref, gk_ref), (dv_ref, gv_ref))):
-            near = near_ref[pl.ds(at, 1), :, :, lanes].astype(F32)
-            far = far_ref[pl.ds(at, 1), :, :, lanes].astype(F32)
-            out[:, :, :, lanes] = (own[:, :, :, lanes] + (near + far)).astype(BF16)
-        moves = [(dqc_ref, dq_hbm), (dkc_ref, dkc_hbm), (gk_ref, gk_hbm), (gv_ref, gv_hbm)]
-        copies.extend(send(pair, moves, sems))
-
+
+    for at, (own, out, hbm) in enumerate(((dk_ref, gk_ref, gk_hbm), (dv_ref, gv_ref, gv_hbm))):
+        rims = near_ref[pl.ds(at, 1)].astype(F32) + far_ref[pl.ds(at, 1)].astype(F32)
+        out[...] = (own[...] + rims).astype(BF16)
+        copies.append(pltpu.make_async_copy(out, hbm, sems.at[1 + at]))
+        copies[-1].start()
     pipelined(products, scores, grads)
+    for at, (out, hbm) in enumerate(((dqc_ref, dq_hbm), (dkc_ref, dkc_hbm))):
+        copies.append(pltpu.make_async_copy(out, hbm, sems.at[3 + at]))
+        copies[-1].start()
     for copy in copies:
         copy.wait()
 
 
 def halo(near, own, far, at, pair):
-    return jnp.concatenate([tokens(r.at[pl.ds(at, 1)], pair) for r in (near, own, far)], axis=0)
+    parts = (near, own.at[pl.ds(at, 1)], far.at[pl.ds(at, 1)])
+    return jnp.concatenate([tokens(part, pair) for part in parts], axis=0)
 
 
 def level_kernel(
-    q_ref, both_ref, near_ref, far_ref, g_ref, bias_ref,
+    q_ref, both_ref, near_k, near_v, far_ref, g_ref, bias_ref,
     dq_ref, att_ref, dk_ref, dv_ref, near_out, far_out,
     s_ref, dp_ref, p_ref, ds_ref, qg_ref, kv_ref,
 ):
@@ -185,8 +176,8 @@
     def products(pair):
         queries = both_heads(tokens(q_ref, pair) * BF16(0.125))
         grads = both_heads(tokens(g_ref, pair))
-        keys = halo(near_ref, both_ref, far_ref, 0, pair)
-        values = halo(near_ref, both_ref, far_ref, 1, pair)
+        keys = halo(near_k, both_ref, far_ref, 0, pair)
+        values = halo(near_v, both_ref, far_ref, 1, pair)
         s_ref[pair % 2] = outer(keys, queries) + bias
         dp_ref[pair % 2] = outer(values, grads)
         qg_ref[pair % 4, 0] = queries
@@ -254,6 +245,8 @@
     given = [
         block_lists, query_column, key_column, grad_output, key_level, value_level, query_level,
     ]
+    near_k = lax.ppermute(key_level, "lon", near)
+    near_v = lax.ppermute(value_level, "lon", near)
     grad_col, both, queries, col_queries, col_keys, col_grads, probs, bias = call(
         column_forward,
         [held(a) for a in (column, two, level, column, column, column, col_probs, mask)],
@@ -266,13 +259,13 @@
             pltpu.SemaphoreType.DMA((7,)),
         ],
     )
-    both_near = lax.ppermute(both, "lon", near)
-    both_far = lax.ppermute(both, "lon", far)
+    shared, near_k, near_v = lax.optimization_barrier((both, near_k, near_v))
+    both_far = lax.ppermute(shared, "lon", far)
     grad_att = lax.all_to_all(grad_col, "lev", split_axis=0, concat_axis=1, tiled=True)
     grad_query, attended, dk, dv, near_terms, far_terms = call(
         level_kernel,
         [held(a) for a in (level, level, level32, level32, two, two)],
-        [queries, both, both_near, both_far, grad_att, bias],
+        [queries, both, near_k, near_v, both_far, grad_att, bias],
         18,
         scratch=[
             pltpu.VMEM((2, 3 * ROWS, 2 * ROWS), F32),
@@ -298,7 +291,7 @@
         scratch=[pltpu.VMEM(column.shape, BF16)] * 2
         + [pltpu.VMEM(level.shape, BF16)] * 2
         + [pltpu.VMEM((2, ROWS, 2 * ROWS), F32), pltpu.VMEM((2, ROWS, 2 * ROWS), BF16)]
-        + [pltpu.SemaphoreType.DMA((4, PAIRS)), pltpu.SemaphoreType.DMA((1,))],
+        + [pltpu.SemaphoreType.DMA((5,))],
     )
     return grad_query, grad_key, grad_value, grad_query_column, grad_key_column
 

time: 45.4 us -> 44.7 us (0.985)
  blocking collectives: 27.4 us -> 26.6 us
    ppermute x1, starting transfers between devices: 1.24 us -> 5.75 us  [on_device(): near_sums = lax.ppermute(near_terms, 'lon', near)]
    ppermute x2 -> x3, starting transfers between devices: 7.9 us -> 3.71 us  [the longest x1 3.33 us: on_device(): near_k = lax.ppermute(key_level, 'lon', near)]
    all_to_all x1, blocking collectives: 13.1 us -> 12.4 us  [on_device(): lax.all_to_all(attended, 'lev', split_axis=1, concat_axis=0, tiled=True)]
  transfers between devices with their start and end apart: 4 -> 5, of which waited for: 0 -> 0; matrix products, arithmetic and copies ran while one was open for 0% -> 0% of each run, Pallas kernels for 0% -> 5%
where the time goes in v5:
time: 44.7 us; the launch traced here: 44.5 us
  blocking collectives  26.6 us (60%)
  starting transfers between devices  9.46 us (21%)
  Pallas kernels  7.77 us (17%)
  between operations  0.67 us (1%)
    all_to_all x1, blocking collectives, on_device(): lax.all_to_all(grad_col, 'lev', split_axis=0, concat_axis=1, tiled=True)  14.2 us
    all_to_all x1, blocking collectives, on_device(): lax.all_to_all(attended, 'lev', split_axis=1, concat_axis=0, tiled=True)  12.4 us
    pallas_call x3, Pallas kernels, call(): pl.pallas_call(kernel, out_shape=outs, in_specs=in_specs or [VMEM] * len(...  7.77 us
    ppermute x1, starting transfers between devices, on_device(): near_sums = lax.ppermute(near_terms, 'lon', near)  5.75 us
    ppermute x1, starting transfers between devices, on_device(): near_k = lax.ppermute(key_level, 'lon', near)  3.33 us
  transfers between devices with their start and end apart: 5, of which 0 were waited for; matrix products, arithmetic and copies ran while one was open for 0% of the time, Pallas kernels for 5%

profile of v5, /device:TPU:1, one launch (start us, length us, event | category | flops | bytes accessed | tf_op | source)
XLA Modules:
  0.0 44.5 jit_solution(17262333025193152366)
XLA Ops:
  0.6 3.3 %collective-permute-start = (bf16[1,32,4,1024]{3,2,1,0:T(4,128)(2,1)}, bf16[1,32,4,1024]{3,2,1,0:T(4,128)(2,1)S(1)}, u32[]{:S(2)}, u32[]{:S(2)}) collective-permute-start(bf16[1,32,4,1024]{3,2,1,0:T(4,128)(2,1)} %lk_hbm.1), channel_id=1, source_target_pairs={{0,8},{8,0},{16,24},{24,16},{32,40},{40,32},{48,56},{56,48},{64,72... | collective-permute-start | bytes 786440 | tf_op jit(solution)/shard_map/ppermute | solution.py:248
  4.0 0.1 collective-permute-start.1
  4.1 2.1 %shard_map.110 = (bf16[8,4,4,1024]{3,2,1,0:T(4,128)(2,1)S(1)}, bf16[2,32,4,1024]{3,2,1,0:T(4,128)(2,1)S(1)}, bf16[1,32,4,1024]{3,2,1,0:T(4,128)(2,1)S(1)}, bf16[...) custom-call(s32[1,4,15]{2,1,0:T(4,128)} %lists_hbm.1, ...), custom_call_target="tpu_custom_call" | custom-call | flops 134217728 | bytes 1573104 | tf_op jit(solution)/shard_map/pallas_call | solution.py:220
  6.1 0.0 collective-permute-done.near_k
  6.1 0.0 collective-permute-done.1.near_v
  6.2 0.3 collective-permute-start.2
  6.4 14.2 %all_to_all.24 = bf16[8,4,4,1024]{3,2,1,0:T(4,128)(2,1)S(1)} all-to-all(bf16[8,4,4,1024]{3,2,1,0:T(4,128)(2,1)S(1)} %get-tuple-element.36), channel_id=1, replica_groups=mesh['lon'=32,'lev'=8] {'lev'}, dimensions={0} | all-to-all | bytes 524288 | tf_op jit(solution)/shard_map/all_to_all | solution.py:264
  20.7 0.0 collective-permute-done.2.far_ref
  20.7 3.5 %shard_map.111 = (bf16[1,32,4,1024]{3,2,1,0:T(4,128)(2,1)S(1)}, bf16[1,32,4,1024]{3,2,1,0:T(4,128)(2,1)S(1)}, f32[1,32,4,1024]{3,2,1,0:T(4,128)S(1)}, f32[1,32,4...) custom-call(bf16[1,32,4,1024]{3,2,1,0:T(4,128)(2,1)S(1)} %get-tuple-element.31.q_ref, ...), custom_call_target="tpu_custom_call" | custom-call | flops 603979776 | bytes 2293760 | tf_op jit(solution)/shard_map/pallas_call | solution.py:220
  24.2 5.7 %collective-permute-start.3 = (bf16[2,32,4,1024]{3,2,1,0:T(4,128)(2,1)S(1)}, bf16[2,32,4,1024]{3,2,1,0:T(4,128)(2,1)S(1)}, u32[]{:S(2)}, u32[]{:S(2)}) collective-permute-start(bf16[2,32,4,1024]{3,2,1,0:T(4,128)(2,1)S(1)} %get-tuple-element.41), channel_id=1, source_target_pairs={{0,8},{8,0},{16,24},{24,16},{32,40},{40,32},{48,56},{56,48},{64,72... | collective-permute-start | bytes 1572872 | tf_op jit(solution)/shard_map/ppermute | solution.py:280
  29.9 0.0 collective-permute-start.4
  29.9 12.4 %all_to_all.25 = bf16[1,32,4,1024]{3,2,0,1:T(4,128)(2,1)S(1)} all-to-all(bf16[1,32,4,1024]{3,2,0,1:T(4,128)(2,1)S(1)} %bitcast.5), channel_id=1, replica_groups=mesh['lon'=32,'lev'=8] {'lev'}, dimensions={1} | all-to-all | bytes 524288 | tf_op jit(solution)/shard_map/all_to_all | solution.py:281
  42.3 0.0 collective-permute-done.3.near_ref
  42.3 0.0 collective-permute-done.4.far_ref
  42.3 2.2 %shard_map.112 = (bf16[8,4,4,1024]{3,2,1,0:T(4,128)(2,1)}, bf16[8,4,4,1024]{3,2,1,0:T(4,128)(2,1)}, bf16[1,32,4,1024]{3,2,1,0:T(4,128)(2,1)}, bf16[1,32,4,1024]{3,2,1,0:T(4,128)(2,1)}, bf16[1,32,4,1024]{3,2,1,0:T(4,128)(2,1)}) custom-call(bf16[8,4,4,1024]{3,2,1,0:T(4,128)(2,1)S(1)} %get-tuple-element.27.q_ref, ...), custom_call_target="tpu_custom_call" | custom-call | flops 268435456 | bytes 4456448 | tf_op jit(solution)/shard_map/pallas_call | solution.py:220
Async XLA Ops:
  0.6 5.5 %collective-permute-start = (bf16[1,32,4,1024]{3,2,1,0:T(4,128)(2,1)}, bf16[1,32,4,1024]{3,2,1,0:T(4,128)(2,1)S(1)}, u32[]{:S(2)}, u32[]{:S(2)}) collective-permute-start(bf16[1,32,4,1024]{3,2,1,0:T(4,128)(2,1)} %lk_hbm.1), channel_id=1, source_target_pairs={{0,8},{8,0},{16,24},{24,16},{32,40},{40,32},{48,56},{56,48},{64,72... | collective-permute-start | bytes 786440 | tf_op jit(solution)/shard_map/ppermute | solution.py:248
  4.0 2.2 %collective-permute-start.1 = (bf16[1,32,4,1024]{3,2,1,0:T(4,128)(2,1)}, bf16[1,32,4,1024]{3,2,1,0:T(4,128)(2,1)S(1)}, u32[]{:S(2)}, u32[]{:S(2)}) collective-permute-start(bf16[1,32,4,1024]{3,2,1,0:T(4,128)(2,1)} %lv_hbm.1), channel_id=1, source_target_pairs={{0,8},{8,0},{16,24},{24,16},{32,40},{40,32},{48,56},{56,48},{64,72... | collective-permute-start | bytes 786440 | tf_op jit(solution)/shard_map/ppermute | solution.py:249
  6.2 14.5 %collective-permute-start.2 = (bf16[2,32,4,1024]{3,2,1,0:T(4,128)(2,1)S(1)}, bf16[2,32,4,1024]{3,2,1,0:T(4,128)(2,1)S(1)}, u32[]{:S(2)}, u32[]{:S(2)}) collective-permute-start(bf16[2,32,4,1024]{3,2,1,0:T(4,128)(2,1)S(1)} %get-tuple-element.35.both_ref), channel_id=1, source_target_pairs={{0,248},{8,16},{16,8},{24,32},{32,24},{40,48},{48,40},{56,64},{64,... | collective-permute-start | bytes 1572872 | tf_op jit(solution)/shard_map/ppermute | solution.py:263
  24.2 18.1 %collective-permute-start.3 = (bf16[2,32,4,1024]{3,2,1,0:T(4,128)(2,1)S(1)}, bf16[2,32,4,1024]{3,2,1,0:T(4,128)(2,1)S(1)}, u32[]{:S(2)}, u32[]{:S(2)}) collective-permute-start(bf16[2,32,4,1024]{3,2,1,0:T(4,128)(2,1)S(1)} %get-tuple-element.41), channel_id=1, source_target_pairs={{0,8},{8,0},{16,24},{24,16},{32,40},{40,32},{48,56},{56,48},{64,72... | collective-permute-start | bytes 1572872 | tf_op jit(solution)/shard_map/ppermute | solution.py:280
  29.9 12.4 %collective-permute-start.4 = (bf16[2,32,4,1024]{3,2,1,0:T(4,128)(2,1)S(1)}, bf16[2,32,4,1024]{3,2,1,0:T(4,128)(2,1)S(1)}, u32[]{:S(2)}, u32[]{:S(2)}) collective-permute-start(bf16[2,32,4,1024]{3,2,1,0:T(4,128)(2,1)S(1)} %get-tuple-element.42), channel_id=1, source_target_pairs={{0,248},{8,16},{16,8},{24,32},{32,24},{40,48},{48,40},{56,64},{64,... | collective-permute-start | bytes 1572872 | tf_op jit(solution)/shard_map/ppermute | solution.py:279

commit v6 on v5

--- a/solution.py
+++ b/solution.py
@@ -148,14 +148,23 @@
         grad_query = own_features(inner(tokens(k_ref, pair).T, d_scores)) * 0.125
         put(dqc_ref, pair, grad_query.astype(BF16).T)
 
-    for at, (own, out, hbm) in enumerate(((dk_ref, gk_ref, gk_hbm), (dv_ref, gv_ref, gv_hbm))):
-        rims = near_ref[pl.ds(at, 1)].astype(F32) + far_ref[pl.ds(at, 1)].astype(F32)
-        out[...] = (own[...] + rims).astype(BF16)
+    def sums(chunk):
+        at, rows = chunk % 2, pl.ds(chunk // 2 * 8, 8)
+        own, out, hbm = ((dk_ref, gk_ref, gk_hbm), (dv_ref, gv_ref, gv_hbm))[at]
+        rims = near_ref[pl.ds(at, 1), rows].astype(F32) + far_ref[pl.ds(at, 1), rows].astype(F32)
+        out[:, rows] = (own[:, rows] + rims).astype(BF16)
+        copies.append(
+            pltpu.make_async_copy(out.at[:, rows], hbm.at[:, rows], sems.at[3 + chunk])
+        )
+        copies[-1].start()
+
+    def products_and_sums(pair):
+        products(pair)
+        sums(pair)
+
+    pipelined(products_and_sums, scores, grads)
+    for at, (out, hbm) in enumerate(((dqc_ref, dq_hbm), (dkc_ref, dkc_hbm))):
         copies.append(pltpu.make_async_copy(out, hbm, sems.at[1 + at]))
-        copies[-1].start()
-    pipelined(products, scores, grads)
-    for at, (out, hbm) in enumerate(((dqc_ref, dq_hbm), (dkc_ref, dkc_hbm))):
-        copies.append(pltpu.make_async_copy(out, hbm, sems.at[3 + at]))
         copies[-1].start()
     for copy in copies:
         copy.wait()
@@ -291,7 +300,7 @@
         scratch=[pltpu.VMEM(column.shape, BF16)] * 2
         + [pltpu.VMEM(level.shape, BF16)] * 2
         + [pltpu.VMEM((2, ROWS, 2 * ROWS), F32), pltpu.VMEM((2, ROWS, 2 * ROWS), BF16)]
-        + [pltpu.SemaphoreType.DMA((5,))],
+        + [pltpu.SemaphoreType.DMA((3 + PAIRS,))],
     )
     return grad_query, grad_key, grad_value, grad_query_column, grad_key_column
 

time: 44.7 us -> 44.5 us (level)
  no operation moved by 1% of the time
where the time goes in v6:
time: 44.5 us; the launch traced here: 44.4 us
  blocking collectives  26.6 us (60%)
  starting transfers between devices  9.46 us (21%)
  Pallas kernels  7.62 us (17%)
  between operations  0.67 us (2%)
    all_to_all x1, blocking collectives, on_device(): lax.all_to_all(grad_col, 'lev', split_axis=0, concat_axis=1, tiled=True)  14.2 us
    all_to_all x1, blocking collectives, on_device(): lax.all_to_all(attended, 'lev', split_axis=1, concat_axis=0, tiled=True)  12.4 us
    pallas_call x3, Pallas kernels, call(): pl.pallas_call(kernel, out_shape=outs, in_specs=in_specs or [VMEM] * len(...  7.62 us
    ppermute x1, starting transfers between devices, on_device(): near_sums = lax.ppermute(near_terms, 'lon', near)  5.75 us
    ppermute x1, starting transfers between devices, on_device(): near_k = lax.ppermute(key_level, 'lon', near)  3.33 us
  transfers between devices with their start and end apart: 5, of which 0 were waited for; matrix products, arithmetic and copies ran while one was open for 0% of the time, Pallas kernels for 5%

profile of v6, /device:TPU:1, one launch (start us, length us, event | category | flops | bytes accessed | tf_op | source)
XLA Modules:
  0.0 44.4 jit_solution(16486246874305642176)
XLA Ops:
  0.6 3.3 %collective-permute-start = (bf16[1,32,4,1024]{3,2,1,0:T(4,128)(2,1)}, bf16[1,32,4,1024]{3,2,1,0:T(4,128)(2,1)S(1)}, u32[]{:S(2)}, u32[]{:S(2)}) collective-permute-start(bf16[1,32,4,1024]{3,2,1,0:T(4,128)(2,1)} %lk_hbm.1), channel_id=1, source_target_pairs={{0,8},{8,0},{16,24},{24,16},{32,40},{40,32},{48,56},{56,48},{64,72... | collective-permute-start | bytes 786440 | tf_op jit(solution)/shard_map/ppermute | solution.py:257
  4.0 0.1 collective-permute-start.1
  4.1 2.1 %shard_map.110 = (bf16[8,4,4,1024]{3,2,1,0:T(4,128)(2,1)S(1)}, bf16[2,32,4,1024]{3,2,1,0:T(4,128)(2,1)S(1)}, bf16[1,32,4,1024]{3,2,1,0:T(4,128)(2,1)S(1)}, bf16[...) custom-call(s32[1,4,15]{2,1,0:T(4,128)} %lists_hbm.1, ...), custom_call_target="tpu_custom_call" | custom-call | flops 134217728 | bytes 1573104 | tf_op jit(solution)/shard_map/pallas_call | solution.py:229
  6.1 0.0 collective-permute-done.near_k
  6.1 0.0 collective-permute-done.1.near_v
  6.2 0.3 collective-permute-start.2
  6.4 14.2 %all_to_all.24 = bf16[8,4,4,1024]{3,2,1,0:T(4,128)(2,1)S(1)} all-to-all(bf16[8,4,4,1024]{3,2,1,0:T(4,128)(2,1)S(1)} %get-tuple-element.36), channel_id=1, replica_groups=mesh['lon'=32,'lev'=8] {'lev'}, dimensions={0} | all-to-all | bytes 524288 | tf_op jit(solution)/shard_map/all_to_all | solution.py:273
  20.7 0.0 collective-permute-done.2.far_ref
  20.7 3.5 %shard_map.111 = (bf16[1,32,4,1024]{3,2,1,0:T(4,128)(2,1)S(1)}, bf16[1,32,4,1024]{3,2,1,0:T(4,128)(2,1)S(1)}, f32[1,32,4,1024]{3,2,1,0:T(4,128)S(1)}, f32[1,32,4...) custom-call(bf16[1,32,4,1024]{3,2,1,0:T(4,128)(2,1)S(1)} %get-tuple-element.31.q_ref, ...), custom_call_target="tpu_custom_call" | custom-call | flops 603979776 | bytes 2293760 | tf_op jit(solution)/shard_map/pallas_call | solution.py:229
  24.2 5.7 %collective-permute-start.3 = (bf16[2,32,4,1024]{3,2,1,0:T(4,128)(2,1)S(1)}, bf16[2,32,4,1024]{3,2,1,0:T(4,128)(2,1)S(1)}, u32[]{:S(2)}, u32[]{:S(2)}) collective-permute-start(bf16[2,32,4,1024]{3,2,1,0:T(4,128)(2,1)S(1)} %get-tuple-element.41), channel_id=1, source_target_pairs={{0,8},{8,0},{16,24},{24,16},{32,40},{40,32},{48,56},{56,48},{64,72... | collective-permute-start | bytes 1572872 | tf_op jit(solution)/shard_map/ppermute | solution.py:289
  29.9 0.0 collective-permute-start.4
  29.9 12.4 %all_to_all.25 = bf16[1,32,4,1024]{3,2,0,1:T(4,128)(2,1)S(1)} all-to-all(bf16[1,32,4,1024]{3,2,0,1:T(4,128)(2,1)S(1)} %bitcast.5), channel_id=1, replica_groups=mesh['lon'=32,'lev'=8] {'lev'}, dimensions={1} | all-to-all | bytes 524288 | tf_op jit(solution)/shard_map/all_to_all | solution.py:290
  42.3 0.0 collective-permute-done.3.near_ref
  42.3 0.0 collective-permute-done.4.far_ref
  42.3 2.1 %shard_map.112 = (bf16[8,4,4,1024]{3,2,1,0:T(4,128)(2,1)}, bf16[8,4,4,1024]{3,2,1,0:T(4,128)(2,1)}, bf16[1,32,4,1024]{3,2,1,0:T(4,128)(2,1)}, bf16[1,32,4,1024]{3,2,1,0:T(4,128)(2,1)}, bf16[1,32,4,1024]{3,2,1,0:T(4,128)(2,1)}) custom-call(bf16[8,4,4,1024]{3,2,1,0:T(4,128)(2,1)S(1)} %get-tuple-element.27.q_ref, ...), custom_call_target="tpu_custom_call" | custom-call | flops 268435456 | bytes 4456448 | tf_op jit(solution)/shard_map/pallas_call | solution.py:229
Async XLA Ops:
  0.6 5.5 %collective-permute-start = (bf16[1,32,4,1024]{3,2,1,0:T(4,128)(2,1)}, bf16[1,32,4,1024]{3,2,1,0:T(4,128)(2,1)S(1)}, u32[]{:S(2)}, u32[]{:S(2)}) collective-permute-start(bf16[1,32,4,1024]{3,2,1,0:T(4,128)(2,1)} %lk_hbm.1), channel_id=1, source_target_pairs={{0,8},{8,0},{16,24},{24,16},{32,40},{40,32},{48,56},{56,48},{64,72... | collective-permute-start | bytes 786440 | tf_op jit(solution)/shard_map/ppermute | solution.py:257
  4.0 2.2 %collective-permute-start.1 = (bf16[1,32,4,1024]{3,2,1,0:T(4,128)(2,1)}, bf16[1,32,4,1024]{3,2,1,0:T(4,128)(2,1)S(1)}, u32[]{:S(2)}, u32[]{:S(2)}) collective-permute-start(bf16[1,32,4,1024]{3,2,1,0:T(4,128)(2,1)} %lv_hbm.1), channel_id=1, source_target_pairs={{0,8},{8,0},{16,24},{24,16},{32,40},{40,32},{48,56},{56,48},{64,72... | collective-permute-start | bytes 786440 | tf_op jit(solution)/shard_map/ppermute | solution.py:258
  6.2 14.5 %collective-permute-start.2 = (bf16[2,32,4,1024]{3,2,1,0:T(4,128)(2,1)S(1)}, bf16[2,32,4,1024]{3,2,1,0:T(4,128)(2,1)S(1)}, u32[]{:S(2)}, u32[]{:S(2)}) collective-permute-start(bf16[2,32,4,1024]{3,2,1,0:T(4,128)(2,1)S(1)} %get-tuple-element.35.both_ref), channel_id=1, source_target_pairs={{0,248},{8,16},{16,8},{24,32},{32,24},{40,48},{48,40},{56,64},{64,... | collective-permute-start | bytes 1572872 | tf_op jit(solution)/shard_map/ppermute | solution.py:272
  24.2 18.1 %collective-permute-start.3 = (bf16[2,32,4,1024]{3,2,1,0:T(4,128)(2,1)S(1)}, bf16[2,32,4,1024]{3,2,1,0:T(4,128)(2,1)S(1)}, u32[]{:S(2)}, u32[]{:S(2)}) collective-permute-start(bf16[2,32,4,1024]{3,2,1,0:T(4,128)(2,1)S(1)} %get-tuple-element.41), channel_id=1, source_target_pairs={{0,8},{8,0},{16,24},{24,16},{32,40},{40,32},{48,56},{56,48},{64,72... | collective-permute-start | bytes 1572872 | tf_op jit(solution)/shard_map/ppermute | solution.py:289
  29.9 12.4 %collective-permute-start.4 = (bf16[2,32,4,1024]{3,2,1,0:T(4,128)(2,1)S(1)}, bf16[2,32,4,1024]{3,2,1,0:T(4,128)(2,1)S(1)}, u32[]{:S(2)}, u32[]{:S(2)}) collective-permute-start(bf16[2,32,4,1024]{3,2,1,0:T(4,128)(2,1)S(1)} %get-tuple-element.42), channel_id=1, source_target_pairs={{0,248},{8,16},{16,8},{24,32},{32,24},{40,48},{48,40},{56,64},{64,... | collective-permute-start | bytes 1572872 | tf_op jit(solution)/shard_map/ppermute | solution.py:288

commit v7 on v6

--- a/solution.py
+++ b/solution.py
@@ -152,7 +152,7 @@
         at, rows = chunk % 2, pl.ds(chunk // 2 * 8, 8)
         own, out, hbm = ((dk_ref, gk_ref, gk_hbm), (dv_ref, gv_ref, gv_hbm))[at]
         rims = near_ref[pl.ds(at, 1), rows].astype(F32) + far_ref[pl.ds(at, 1), rows].astype(F32)
-        out[:, rows] = (own[:, rows] + rims).astype(BF16)
+        out[:, rows] = (own[:, rows].astype(F32) + rims).astype(BF16)
         copies.append(
             pltpu.make_async_copy(out.at[:, rows], hbm.at[:, rows], sems.at[3 + chunk])
         )
@@ -246,7 +246,6 @@
     near = [(i, i ^ 1) for i in range(size)]
     far = [(i, (i + 1) % size if i % 2 else (i - 1) % size) for i in range(size)]
     level = jax.ShapeDtypeStruct(query_level.shape, BF16)
-    level32 = jax.ShapeDtypeStruct(query_level.shape, F32)
     column = jax.ShapeDtypeStruct(query_column.shape, BF16)
     two = jax.ShapeDtypeStruct((2,) + query_level.shape[1:], BF16)
     col_probs = jax.ShapeDtypeStruct((PAIRS, ROWS, 2 * ROWS), F32)
@@ -273,7 +272,7 @@
     grad_att = lax.all_to_all(grad_col, "lev", split_axis=0, concat_axis=1, tiled=True)
     grad_query, attended, dk, dv, near_terms, far_terms = call(
         level_kernel,
-        [held(a) for a in (level, level, level32, level32, two, two)],
+        [held(a) for a in (level, level, level, level, two, two)],
         [queries, both, near_k, near_v, both_far, grad_att, bias],
         18,
         scratch=[

time: 44.5 us -> 44.6 us (level)
  no operation moved by 1% of the time
where the time goes in v7:
time: 44.6 us; the launch traced here: 44.4 us
  blocking collectives  26.6 us (60%)
  starting transfers between devices  9.47 us (21%)
  Pallas kernels  7.66 us (17%)
  between operations  0.67 us (2%)
    all_to_all x1, blocking collectives, on_device(): lax.all_to_all(grad_col, 'lev', split_axis=0, concat_axis=1, tiled=True)  14.2 us
    all_to_all x1, blocking collectives, on_device(): lax.all_to_all(attended, 'lev', split_axis=1, concat_axis=0, tiled=True)  12.4 us
    pallas_call x3, Pallas kernels, call(): pl.pallas_call(kernel, out_shape=outs, in_specs=in_specs or [VMEM] * len(...  7.66 us
    ppermute x1, starting transfers between devices, on_device(): near_sums = lax.ppermute(near_terms, 'lon', near)  5.75 us
    ppermute x1, starting transfers between devices, on_device(): near_k = lax.ppermute(key_level, 'lon', near)  3.33 us
  transfers between devices with their start and end apart: 5, of which 0 were waited for; matrix products, arithmetic and copies ran while one was open for 0% of the time, Pallas kernels for 5%

profile of v7, /device:TPU:1, one launch (start us, length us, event | category | flops | bytes accessed | tf_op | source)
XLA Modules:
  0.0 44.4 jit_solution(4951221141162082831)
XLA Ops:
  0.6 3.3 %collective-permute-start = (bf16[1,32,4,1024]{3,2,1,0:T(4,128)(2,1)}, bf16[1,32,4,1024]{3,2,1,0:T(4,128)(2,1)S(1)}, u32[]{:S(2)}, u32[]{:S(2)}) collective-permute-start(bf16[1,32,4,1024]{3,2,1,0:T(4,128)(2,1)} %lk_hbm.1), channel_id=1, source_target_pairs={{0,8},{8,0},{16,24},{24,16},{32,40},{40,32},{48,56},{56,48},{64,72... | collective-permute-start | bytes 786440 | tf_op jit(solution)/shard_map/ppermute | solution.py:256
  4.0 0.1 collective-permute-start.1
  4.1 2.1 %shard_map.110 = (bf16[8,4,4,1024]{3,2,1,0:T(4,128)(2,1)S(1)}, bf16[2,32,4,1024]{3,2,1,0:T(4,128)(2,1)S(1)}, bf16[1,32,4,1024]{3,2,1,0:T(4,128)(2,1)S(1)}, bf16[...) custom-call(s32[1,4,15]{2,1,0:T(4,128)} %lists_hbm.1, ...), custom_call_target="tpu_custom_call" | custom-call | flops 134217728 | bytes 1573104 | tf_op jit(solution)/shard_map/pallas_call | solution.py:229
  6.1 0.0 collective-permute-done.near_k
  6.1 0.0 collective-permute-done.1.near_v
  6.2 0.3 collective-permute-start.2
  6.4 14.2 %all_to_all.24 = bf16[8,4,4,1024]{3,2,1,0:T(4,128)(2,1)S(1)} all-to-all(bf16[8,4,4,1024]{3,2,1,0:T(4,128)(2,1)S(1)} %get-tuple-element.36), channel_id=1, replica_groups=mesh['lon'=32,'lev'=8] {'lev'}, dimensions={0} | all-to-all | bytes 524288 | tf_op jit(solution)/shard_map/all_to_all | solution.py:272
  20.7 0.0 collective-permute-done.2.far_ref
  20.7 3.5 %shard_map.111 = (bf16[1,32,4,1024]{3,2,1,0:T(4,128)(2,1)S(1)}, bf16[1,32,4,1024]{3,2,1,0:T(4,128)(2,1)S(1)}, bf16[1,32,4,1024]{3,2,1,0:T(4,128)(2,1)S(1)}, bf16...) custom-call(bf16[1,32,4,1024]{3,2,1,0:T(4,128)(2,1)S(1)} %get-tuple-elem, ...), custom_call_target="tpu_custom_call" | custom-call | flops 603979776 | bytes 2293760 | tf_op jit(solution)/shard_map/pallas_call | solution.py:229
  24.2 5.8 %collective-permute-start.3 = (bf16[2,32,4,1024]{3,2,1,0:T(4,128)(2,1)S(1)}, bf16[2,32,4,1024]{3,2,1,0:T(4,128)(2,1)S(1)}, u32[]{:S(2)}, u32[]{:S(2)}) collective-permute-start(bf16[2,32,4,1024]{3,2,1,0:T(4,128)(2,1)S(1)} %get-tuple-element.41), channel_id=1, source_target_pairs={{0,8},{8,0},{16,24},{24,16},{32,40},{40,32},{48,56},{56,48},{64,72... | collective-permute-start | bytes 1572872 | tf_op jit(solution)/shard_map/ppermute | solution.py:288
  29.9 0.0 collective-permute-start.4
  29.9 12.4 %all_to_all.25 = bf16[1,32,4,1024]{3,2,0,1:T(4,128)(2,1)S(1)} all-to-all(bf16[1,32,4,1024]{3,2,0,1:T(4,128)(2,1)S(1)} %bitcast.5), channel_id=1, replica_groups=mesh['lon'=32,'lev'=8] {'lev'}, dimensions={1} | all-to-all | bytes 524288 | tf_op jit(solution)/shard_map/all_to_all | solution.py:289
  42.3 0.0 collective-permute-done.3.near_ref
  42.3 0.0 collective-permute-done.4.far_ref
  42.3 2.1 %shard_map.112 = (bf16[8,4,4,1024]{3,2,1,0:T(4,128)(2,1)}, bf16[8,4,4,1024]{3,2,1,0:T(4,128)(2,1)}, bf16[1,32,4,1024]{3,2,1,0:T(4,128)(2,1)}, bf16[1,32,4,1024]{3,2,1,0:T(4,128)(2,1)}, bf16[1,32,4,1024]{3,2,1,0:T(4,128)(2,1)}) custom-call(bf16[8,4,4,1024]{3,2,1,0:T(4,128)(2,1)S(1)} %get-tuple-element.27.q_ref, ...), custom_call_target="tpu_custom_call" | custom-call | flops 268435456 | bytes 3932160 | tf_op jit(solution)/shard_map/pallas_call | solution.py:229
Async XLA Ops:
  0.6 5.5 %collective-permute-start = (bf16[1,32,4,1024]{3,2,1,0:T(4,128)(2,1)}, bf16[1,32,4,1024]{3,2,1,0:T(4,128)(2,1)S(1)}, u32[]{:S(2)}, u32[]{:S(2)}) collective-permute-start(bf16[1,32,4,1024]{3,2,1,0:T(4,128)(2,1)} %lk_hbm.1), channel_id=1, source_target_pairs={{0,8},{8,0},{16,24},{24,16},{32,40},{40,32},{48,56},{56,48},{64,72... | collective-permute-start | bytes 786440 | tf_op jit(solution)/shard_map/ppermute | solution.py:256
  4.0 2.2 %collective-permute-start.1 = (bf16[1,32,4,1024]{3,2,1,0:T(4,128)(2,1)}, bf16[1,32,4,1024]{3,2,1,0:T(4,128)(2,1)S(1)}, u32[]{:S(2)}, u32[]{:S(2)}) collective-permute-start(bf16[1,32,4,1024]{3,2,1,0:T(4,128)(2,1)} %lv_hbm.1), channel_id=1, source_target_pairs={{0,8},{8,0},{16,24},{24,16},{32,40},{40,32},{48,56},{56,48},{64,72... | collective-permute-start | bytes 786440 | tf_op jit(solution)/shard_map/ppermute | solution.py:257
  6.2 14.5 %collective-permute-start.2 = (bf16[2,32,4,1024]{3,2,1,0:T(4,128)(2,1)S(1)}, bf16[2,32,4,1024]{3,2,1,0:T(4,128)(2,1)S(1)}, u32[]{:S(2)}, u32[]{:S(2)}) collective-permute-start(bf16[2,32,4,1024]{3,2,1,0:T(4,128)(2,1)S(1)} %get-tuple-element.35.both_ref), channel_id=1, source_target_pairs={{0,248},{8,16},{16,8},{24,32},{32,24},{40,48},{48,40},{56,64},{64,... | collective-permute-start | bytes 1572872 | tf_op jit(solution)/shard_map/ppermute | solution.py:271
  24.2 18.1 %collective-permute-start.3 = (bf16[2,32,4,1024]{3,2,1,0:T(4,128)(2,1)S(1)}, bf16[2,32,4,1024]{3,2,1,0:T(4,128)(2,1)S(1)}, u32[]{:S(2)}, u32[]{:S(2)}) collective-permute-start(bf16[2,32,4,1024]{3,2,1,0:T(4,128)(2,1)S(1)} %get-tuple-element.41), channel_id=1, source_target_pairs={{0,8},{8,0},{16,24},{24,16},{32,40},{40,32},{48,56},{56,48},{64,72... | collective-permute-start | bytes 1572872 | tf_op jit(solution)/shard_map/ppermute | solution.py:288
  29.9 12.4 %collective-permute-start.4 = (bf16[2,32,4,1024]{3,2,1,0:T(4,128)(2,1)S(1)}, bf16[2,32,4,1024]{3,2,1,0:T(4,128)(2,1)S(1)}, u32[]{:S(2)}, u32[]{:S(2)}) collective-permute-start(bf16[2,32,4,1024]{3,2,1,0:T(4,128)(2,1)S(1)} %get-tuple-element.42), channel_id=1, source_target_pairs={{0,248},{8,16},{16,8},{24,32},{32,24},{40,48},{48,40},{56,64},{64,... | collective-permute-start | bytes 1572872 | tf_op jit(solution)/shard_map/ppermute | solution.py:287
